TPU v7x, 32 devices: a whole 2x2x4 slice. The times are simulated.
32 devices in a mesh: tm: 8 (over y, x, core), space: 4 (over z).
Axes of the slice: x: 2, y: 2, z: 4, core: 2. Of those that a mesh axis runs over, the one named last changes fastest.
Arguments:
- eigvecs: bfloat16 [2, 3, 8, 2048, 256], P(None, None, 'tm', 'space'), may hold values from -0.125 to 0.125
- propagator: bfloat16 [2, 3, 8, 2048, 128], P(None, None, 'tm', 'space'), may hold values from -6 to 6
- elementals: bfloat16 [8, 8, 2, 256, 256], P('tm'), may hold values from -0.0017089844 to 0.0017089844
- sink_times: int32 [8, 16], P('tm'), may hold values from 0 to 7, as said below
- momenta: int32 [8, 16], P('tm'), may hold values from 0 to 7
Outputs:
- traces: float32 [2, 8, 16], P(None, 'tm')
Inputs may be any that keep to these rules, and one draw needn't show every extreme that they name: (sink_times[t, k] - t) modulo 8 lies in 0 to 5 or equals 7; item 0 of every slice t has sink time (t + 4) modulo 8, item 1 has (t - 1) modulo 8.
All inputs are finite; a program needn't handle non-finite values.
Results may differ from a plain program's by a relative error of at most 0.0049.
Values may be sent and summed in bfloat16 or wider, within the bound.
No kernel may reach another device: no remote copies, remote signals or barrier semaphores. Data moves between devices by JAX's collectives and lax.ppermute only.
A program may use at most 64 MiB of HBM per device.

v0:
```python
import jax
import jax.numpy as jnp
from jax import lax
from jax.sharding import PartitionSpec as P


def on_device(eigvecs, propagator, elementals, sink_times, momenta):
    vec_count = eigvecs.shape[-1]
    column_count = propagator.shape[-1]
    momentum_count = elementals.shape[1]
    vecs_flat = eigvecs.reshape(2, -1, vec_count)
    columns_both = jnp.concatenate([vecs_flat[0], vecs_flat[1]], axis=0)
    columns_swap = jnp.concatenate([-vecs_flat[1], vecs_flat[0]], axis=0)
    vec_both = jnp.stack([columns_both, columns_swap], axis=1)
    prop_cat = propagator.reshape(-1, column_count)
    moments = elementals[0]
    own_block = lax.psum_scatter(
        lax.dot_general(
            prop_cat, vec_both, (((0,), (0,)), ((), ())), preferred_element_type=jnp.float32
        ),
        "space",
        scatter_dimension=0,
        tiled=True,
    ).astype(jnp.bfloat16)
    expand = jnp.einsum("prab,sqb->prsqa", moments, own_block, preferred_element_type=jnp.float32)
    real_part = expand[:, 0, :, 0] - expand[:, 1, :, 1]
    imag_part = expand[:, 0, :, 1] + expand[:, 1, :, 0]
    mixed_terms = jnp.stack([real_part, imag_part], axis=2).astype(jnp.bfloat16)
    swapped = jnp.stack([mixed_terms[:, :, 1], -mixed_terms[:, :, 0]], axis=2)
    weights = jnp.stack([mixed_terms, swapped], axis=1).reshape(2 * momentum_count, -1)
    time_slots = lax.axis_size("tm")
    pick_mom = (momenta[0][:, None] == jnp.arange(momentum_count, dtype=jnp.int32)[None, :]).astype(
        jnp.float32
    )
    blocks = lax.all_gather(own_block[None], "tm", axis=0, tiled=True)
    flattened = blocks.reshape(blocks.shape[0], -1)
    values = lax.dot_general(
        weights, flattened, (((1,), (1,)), ((), ())), preferred_element_type=jnp.float32
    )
    tables = values
    slot_index = sink_times[0]
    tables = tables.reshape(momentum_count, 2, time_slots)
    pick_time = (slot_index[:, None] == jnp.arange(time_slots, dtype=jnp.int32)[None, :]).astype(
        jnp.float32
    )
    spread = jnp.einsum("kp,pot->okt", pick_mom, tables, precision=lax.Precision.HIGHEST)
    picked = jnp.sum(spread * pick_time[None], axis=2)
    summed = lax.psum(picked, "space")
    return summed[:, None, :]


def solution(mesh):
    return jax.shard_map(
        on_device,
        mesh=mesh,
        in_specs=(
            P(None, None, "tm", "space", None),
            P(None, None, "tm", "space", None),
            P("tm", None, None, None, None),
            P("tm", None),
            P("tm", None),
        ),
        out_specs=P(None, "tm", None),
        check_vma=False,
    )
```

profile of v0, /device:TPU:0, one launch (start us, length us, event | category | flops | bytes accessed | tf_op | source)
XLA Modules:
  0.0 58.7 jit_solution(13672944883100855210)
XLA Ops:
  0.0 0.0 copy-start
  0.0 2.8 %fusion.27 = (bf16[1,3,1,512,256]{4,3,1,2,0:T(8,128)(2,1)}, bf16[1,3,1,512,256]{4,3,1,2,0:T(8,128)(2,1)}) fusion(bf16[2,3,1,512,256]{4,3,1,2,0:T(8,128)(2,1)} %bitcast.67), kind=kLoop, calls=%fused_computation.34 | loop fusion | bytes 3145728 | tf_op jit(solution)/shard_map/slice | solution.py:12
  2.8 1.4 %copy.28 = bf16[1536,256]{0,1:T(8,128)(2,1)S(1)} copy(bf16[1536,256]{1,0:T(8,128)(2,1)} %bitcast.66) | data formatting | bytes 1572864 | tf_op jit(solution)/shard_map/squeeze | solution.py:12
  4.2 1.0 %neg.7 = bf16[1536,256]{0,1:T(8,128)(2,1)} negate(bf16[1536,256]{0,1:T(8,128)(2,1)S(1)} %copy.28) | non-fusion elementwise | flops 393216 | bytes 1572864 | tf_op jit(solution)/shard_map/neg | solution.py:13
  5.2 2.3 %copy.27 = bf16[1536,256]{0,1:T(8,128)(2,1)} copy(bf16[1536,256]{1,0:T(8,128)(2,1)} %bitcast.65) | data formatting | bytes 1572864 | tf_op jit(solution)/shard_map/squeeze | solution.py:12
  7.5 0.0 copy-start.3
  7.5 2.1 %maximum_bitcast_fusion = (bf16[3072,1,256]{0,2,1:T(8,128)(2,1)S(1)}, bf16[3072,1,256]{0,2,1:T(8,128)(2,1)S(1)}) fusion(bf16[1536,256]{0,1:T(8,128)(2,1)S(1)} %copy.28, bf16[1536,256]{0,1:T(8,128)(2,1)} %copy.27, bf16[1536,256]{0,1:T(8,128)(2,1)} %neg.7), kind=kLoop, calls=%fused_computation.6 | loop fusion | flops 6291456 | bytes 5505024 | tf_op jit(solution)/shard_map/stack | solution.py:14
  9.6 0.0 copy-done.3
  9.6 0.0 copy-start.4
  9.6 1.0 %fusion.9 = f32[128,2,256]{0,2,1:T(8,128)S(1)} fusion(bf16[3072,128,1]{1,0,2:T(8,128)(2,1)S(1)} %bitcast.72, bf16[3072,1,256]{0,2,1:T(8,128)(2,1)S(1)} %get-tuple-element.10, bf16[3072,1,256]{0,2,1:T(8,128)(2,1)S(1)} %get-tuple-element.9), kind=kOutput, calls=%fused_computation.9 | convolution fusion | flops 404226048 | bytes 4194304 | tf_op jit(solution)/shard_map/dot_general | solution.py:18
  10.6 0.1 copy.31
  10.8 25.9 %all-reduce.2 = bf16[128,2,256]{2,1,0:T(2,128)(2,1)S(1)} all-reduce(f32[128,2,256]{2,1,0:T(2,128)S(1)} %copy.31), channel_id=3, replica_groups=mesh['tm'=8,'space'=4] {'space'}, use_global_device_ids=true, to_apply=%region_0.0.clone | all-reduce | flops 65536 | bytes 393216
  36.6 0.0 copy-done.4
  36.7 0.6 dynamic-slice
  37.9 0.0 copy-done
  37.9 0.7 %fusion.6 = f32[8,2,32,2,256]{4,2,1,0,3:T(8,128)S(1)} fusion(bf16[1,8,2,256,256]{4,3,2,1,0:T(8,128)(2,1)S(1)} %copy-done, bf16[32,2,256,1,1]{2,1,0,4,3:T(2,128)(2,1)S(1)} %fusion.32), kind=kOutput, calls=%fused_computation.8 | convolution fusion | flops 134217728 | bytes 3178496 | tf_op jit(solution)/shard_map/prab,sqb->prsqa/dot_general | solution.py:25
  38.7 0.1 negate_bitcast_fusion
  38.8 0.0 copy-start.2
  38.8 0.0 copy-start.1
  38.9 0.1 pad_maximum_fusion
  39.0 9.3 %all-gather = bf16[256,2,256]{2,1,0:T(2,128)(2,1)S(1)} all-gather(bf16[32,2,256]{2,1,0:T(2,128)(2,1)S(1)} %dynamic-slice_convert_fusion), channel_id=2, replica_groups=mesh['tm'=8,'space'=4] {'tm'}, dimensions={0}, use_global_device_ids=true | all-gather | bytes 294912 | tf_op jit(solution)/shard_map/all_gather | solution.py:35
  48.3 1.3 %convolution_bitcast_fusion.1 = f32[8,2,8]{0,2,1:T(8,128)S(1)} fusion(bf16[8,2,32,2,256]{4,2,0,3,1:T(8,128)(2,1)S(1)} %pad_maximum_fusion, bf16[8,32,2,256]{3,2,1,0:T(2,128)(2,1)S(1)} %bitcast.68), kind=kOutput, calls=%fused_computation.12 | convolution fusion | flops 4194304 | bytes 786944 | tf_op jit(solution)/shard_map/dot_general | solution.py:37
  49.6 0.0 copy-done.2
  49.6 0.0 copy-done.1
  49.6 0.1 fusion.13
  49.7 8.9 %psum.7 = f32[2,1,16]{2,0,1:T(2,128)} all-reduce(f32[2,1,16]{2,0,1:T(2,128)S(1)} %bitcast.69), channel_id=1, replica_groups=mesh['tm'=8,'space'=4] {'space'}, use_global_device_ids=true, to_apply=%region_2.0 | all-reduce | flops 32 | bytes 256 | tf_op jit(solution)/shard_map/psum | solution.py:48
  (6 shorter events, 0.2 us)
Async XLA Ops:
  0.0 37.9 %copy-start = (bf16[1,8,2,256,256]{4,3,2,1,0:T(8,128)(2,1)S(1)}, bf16[1,8,2,256,256]{4,3,2,1,0:T(8,128)(2,1)}, u32[]{:S(2)}) copy-start(bf16[1,8,2,256,256]{4,3,2,1,0:T(8,128)(2,1)} %param.7) | copy-start | bytes 6291460
  7.5 2.1 %copy-start.3 = (bf16[2,3,1,512,128]{4,3,2,1,0:T(8,128)(2,1)S(1)}, bf16[2,3,1,512,128]{4,3,2,1,0:T(8,128)(2,1)}, u32[]{:S(2)}) copy-start(bf16[2,3,1,512,128]{4,3,2,1,0:T(8,128)(2,1)} %param.6) | copy-start | bytes 2359300
  9.6 27.0 %copy-start.4 = (u32[32]{0:T(128)S(1)}, u32[32]{0:T(128)}, u32[]{:S(2)}) copy-start(u32[32]{0:T(128)} %constant.9) | copy-start | bytes 388
  38.8 10.8 %copy-start.2 = (s32[1,16]{1,0:T(1,128)S(1)}, s32[1,16]{1,0:T(1,128)}, u32[]{:S(2)}) copy-start(s32[1,16]{1,0:T(1,128)} %param.8) | copy-start | bytes 196
  38.8 10.8 %copy-start.1 = (s32[1,16]{1,0:T(1,128)S(1)}, s32[1,16]{1,0:T(1,128)}, u32[]{:S(2)}) copy-start(s32[1,16]{1,0:T(1,128)} %param.9) | copy-start | bytes 196
where the time goes:
time: 59 us; the launch traced here: 58.7 us
  blocking collectives  44.1 us (75%)
  local copies, waits for them, and re-layouts  7.33 us (12%)
  other arithmetic  3.3 us (6%)
  matrix products  3.12 us (5%)
  between operations  0.82 us (1%)
    unnamed x1, blocking collectives  25.9 us
    all_gather x1, blocking collectives, on_device(): blocks = lax.all_gather(own_block[None], 'tm', axis=0, tiled=True)  9.32 us
    psum x1, blocking collectives, on_device(): summed = lax.psum(picked, 'space')  8.94 us
    squeeze x2, local copies, waits for them, and re-layouts, on_device(): columns_both = jnp.concatenate([vecs_flat[0], vecs_flat[1]], axis=0)  3.72 us
    slice x1, local copies, waits for them, and re-layouts, on_device(): columns_both = jnp.concatenate([vecs_flat[0], vecs_flat[1]], axis=0)  2.79 us
    another operation x1, other arithmetic, on_device(): vec_both = jnp.stack([columns_both, columns_swap], axis=1)  2.07 us
    dot_general x1, matrix products, on_device(): lax.dot_general(weights, flattened, (((1,), (1,)), ((), ())), preferred_e...  1.26 us

commit v1 on v0

--- a/solution.py
+++ b/solution.py
@@ -1,10 +1,195 @@
+import functools
+
 import jax
 import jax.numpy as jnp
 from jax import lax
+from jax.experimental import pallas as pl
+from jax.experimental.pallas import tpu as pltpu
 from jax.sharding import PartitionSpec as P
 
-
-def on_device(eigvecs, propagator, elementals, sink_times, momenta):
+MIB = 1 << 20
+
+
+def project_kernel(vec_hbm, prop_hbm, keep_ref, send_ref, vec_buf, prop_buf, acc_ref, sems):
+    colours = vec_buf.shape[1]
+    vec_count = vec_buf.shape[-1]
+    columns = prop_buf.shape[-1]
+    half = columns // 2
+    copies = []
+    for c in range(colours):
+        vec_copy = pltpu.make_async_copy(vec_hbm.at[:, c, 0], vec_buf.at[:, c], sems.at[0, c])
+        prop_copy = pltpu.make_async_copy(prop_hbm.at[:, c, 0], prop_buf.at[:, c], sems.at[1, c])
+        prop_copy.start()
+        vec_copy.start()
+        copies.append((vec_copy, prop_copy))
+    for c in range(colours):
+        for copy in copies[c]:
+            copy.wait()
+        lhs = jnp.concatenate([prop_buf[0, c], prop_buf[1, c]], axis=-1)
+        rhs = jnp.concatenate([vec_buf[0, c], vec_buf[1, c]], axis=-1)
+        part = lax.dot_general(
+            lhs, rhs, (((0,), (0,)), ((), ())), preferred_element_type=jnp.float32
+        )
+        if c == 0:
+            acc_ref[...] = part
+        else:
+            acc_ref[...] += part
+    mine = lax.rem(lax.axis_index("space"), 2)
+    for out_ref, which in ((send_ref, 1 - mine), (keep_ref, mine)):
+        top = pl.ds(pl.multiple_of(which * half, half), half)
+        low = pl.ds(pl.multiple_of(columns + which * half, half), half)
+        out_ref[0] = acc_ref[top, :vec_count] + acc_ref[low, vec_count:]
+        out_ref[1] = acc_ref[low, :vec_count] - acc_ref[top, vec_count:]
+
+
+def project(eigvecs, propagator):
+    _, colours, _, sites, vec_count = eigvecs.shape
+    columns = propagator.shape[-1]
+    out = jax.ShapeDtypeStruct((2, columns // 2, vec_count), jnp.float32)
+    return pl.pallas_call(
+        project_kernel,
+        out_shape=(out, out),
+        in_specs=[pl.BlockSpec(memory_space=pl.ANY)] * 2,
+        out_specs=[pl.BlockSpec(memory_space=pltpu.VMEM)] * 2,
+        scratch_shapes=[
+            pltpu.VMEM((2, colours, sites, vec_count), jnp.bfloat16),
+            pltpu.VMEM((2, colours, sites, columns), jnp.bfloat16),
+            pltpu.VMEM((2 * columns, 2 * vec_count), jnp.float32),
+            pltpu.SemaphoreType.DMA((2, colours)),
+        ],
+        compiler_params=pltpu.CompilerParams(vmem_limit_bytes=16 * MIB),
+        name="project",
+    )(eigvecs, propagator)
+
+
+def mix_kernel(own_ref, other_ref, elem_ref, mixed_ref):
+    momenta = elem_ref.shape[1]
+    half = own_ref.shape[1]
+    full = (own_ref[...] + other_ref[...]).astype(jnp.bfloat16)
+    both = full.reshape(2 * half, full.shape[-1])
+    for p in range(momenta):
+        by_real, by_imag = (
+            lax.dot_general(
+                both, elem_ref[0, p, r], (((1,), (1,)), ((), ())), preferred_element_type=jnp.float32
+            )
+            for r in range(2)
+        )
+        mixed_ref[p, 0] = (by_real[:half] - by_imag[half:]).astype(jnp.bfloat16)
+        mixed_ref[p, 1] = (by_imag[:half] + by_real[half:]).astype(jnp.bfloat16)
+
+
+def mix(own, other, elementals):
+    momenta = elementals.shape[1]
+    size = own.size
+    return pl.pallas_call(
+        mix_kernel,
+        out_shape=jax.ShapeDtypeStruct((momenta,) + own.shape, jnp.bfloat16),
+        in_specs=[pl.BlockSpec(memory_space=pltpu.VMEM)] * 3,
+        out_specs=pl.BlockSpec(memory_space=pltpu.VMEM),
+        compiler_params=pltpu.CompilerParams(vmem_limit_bytes=16 * MIB),
+        cost_estimate=pl.CostEstimate(
+            flops=4 * momenta * size * own.shape[-1], bytes_accessed=8 * size, transcendentals=0
+        ),
+        name="mix",
+    )(own, other, elementals)
+
+
+def trace_kernel(orders, sink_ref, mom_ref, mixed_ref, *refs):
+    groups, out_ref, sums_ref = refs[:-2], refs[-2], refs[-1]
+    items = out_ref.shape[1]
+    own_slice = lax.axis_index("tm")
+    own_core = own_slice & 1
+
+    def one(k, carry):
+        p = mom_ref[0, k]
+        away = sink_ref[0, k] ^ own_slice
+        crossed = away & 1
+        holder = own_core ^ crossed
+        slots = []
+        for order in orders:
+            slot = 0
+            for place, bit in enumerate(order):
+                slot = slot + (((away >> bit) & 1) << place)
+            slots.append(slot)
+        slot = jnp.where(holder == 0, slots[0], slots[1])
+        late = slot >> (len(orders[0]) - 1)
+        inner = slot & ((1 << (len(orders[0]) - 1)) - 1)
+        group = crossed * 2 + late
+        mixed_real = mixed_ref[p, 0].astype(jnp.float32)
+        mixed_imag = mixed_ref[p, 1].astype(jnp.float32)
+        for g, ref in enumerate(groups):
+
+            @pl.when(group == g)
+            def _(ref=ref):
+                real = ref[inner, 0].astype(jnp.float32)
+                imag = ref[inner, 1].astype(jnp.float32)
+                for o, value in enumerate(
+                    (mixed_real * real + mixed_imag * imag, mixed_imag * real - mixed_real * imag)
+                ):
+                    rows, lanes = value.shape
+                    value = jnp.sum(value.reshape(rows // 8, 8, lanes), axis=0)
+                    value = sum(value[:, i * 128 : (i + 1) * 128] for i in range(lanes // 128))
+                    sums_ref[o, k] = value
+
+        return carry
+
+    lax.fori_loop(0, items, one, 0)
+    out_ref[...] = jnp.sum(sums_ref[...], axis=2)
+
+
+def trace(orders, sink_times, momenta, mixed, groups):
+    items = sink_times.shape[1]
+    return pl.pallas_call(
+        functools.partial(trace_kernel, orders),
+        out_shape=jax.ShapeDtypeStruct((2, items, 128), jnp.float32),
+        in_specs=[pl.BlockSpec(memory_space=pltpu.SMEM)] * 2
+        + [pl.BlockSpec(memory_space=pltpu.VMEM)] * (1 + len(groups)),
+        out_specs=pl.BlockSpec(memory_space=pltpu.VMEM),
+        scratch_shapes=[pltpu.VMEM((2, items, 8, 128), jnp.float32)],
+        compiler_params=pltpu.CompilerParams(vmem_limit_bytes=16 * MIB),
+        name="trace",
+    )(sink_times, momenta, mixed, *groups)
+
+
+def by_exchanges(slice_count, space_count, eigvecs, propagator, elementals, sink_times, momenta):
+    axes = ("tm", "space")
+    slice_bits = slice_count.bit_length() - 1
+    space_bits = space_count.bit_length() - 1
+    orders = (tuple(range(1, slice_bits)), tuple(range(slice_bits - 1, 0, -1)))
+
+    def exchange(value, partner):
+        pairs = []
+        for t in range(slice_count):
+            for s in range(space_count):
+                to_t, to_s = partner(t, s)
+                pairs.append((t * space_count + s, to_t * space_count + to_s))
+        return lax.ppermute(value, axes, pairs)
+
+    def across(value, bit):
+        return exchange(value, lambda t, s: (t, s ^ (1 << bit)))
+
+    keep, send = project(eigvecs, propagator)
+    own = keep + across(send, 0)
+    blocks = own.astype(jnp.bfloat16)[None]
+    total, other = own, jnp.zeros_like(own)
+    for bit in range(1, space_bits):
+        if bit > 1:
+            total = total + other
+        other = across(total, bit)
+    for step in range(slice_bits - 1):
+        arrived = exchange(blocks, lambda t, s: (t ^ (1 << orders[t & 1][step]), s))
+        if step < slice_bits - 2:
+            blocks = jnp.concatenate([blocks, arrived], axis=0)
+    cross = lambda t, s: (t ^ 1, s)
+    groups = [blocks, arrived, exchange(blocks, cross), exchange(arrived, cross)]
+    mixed = mix(total, other, elementals)
+    partial = trace(orders, sink_times, momenta, mixed, groups)
+    for bit in range(space_bits):
+        partial = partial + across(partial, bit)
+    return jnp.sum(partial, axis=-1)[:, None, :]
+
+
+def by_collectives(eigvecs, propagator, elementals, sink_times, momenta):
     vec_count = eigvecs.shape[-1]
     column_count = propagator.shape[-1]
     momentum_count = elementals.shape[1]
@@ -34,10 +219,9 @@
     )
     blocks = lax.all_gather(own_block[None], "tm", axis=0, tiled=True)
     flattened = blocks.reshape(blocks.shape[0], -1)
-    values = lax.dot_general(
+    tables = lax.dot_general(
         weights, flattened, (((1,), (1,)), ((), ())), preferred_element_type=jnp.float32
     )
-    tables = values
     slot_index = sink_times[0]
     tables = tables.reshape(momentum_count, 2, time_slots)
     pick_time = (slot_index[:, None] == jnp.arange(time_slots, dtype=jnp.int32)[None, :]).astype(
@@ -49,7 +233,16 @@
     return summed[:, None, :]
 
 
+def power_of_two(count):
+    return count & (count - 1) == 0
+
+
 def solution(mesh):
+    slice_count, space_count = mesh.shape["tm"], mesh.shape["space"]
+    on_device = by_collectives
+    if power_of_two(slice_count) and power_of_two(space_count):
+        if slice_count > 4 and space_count > 2:
+            on_device = functools.partial(by_exchanges, slice_count, space_count)
     return jax.shard_map(
         on_device,
         mesh=mesh,

time: 59 us -> 35.4 us (0.60)
  blocking collectives: 44.1 us -> 0 us
  waiting for transfers between devices: 0 us -> 16.5 us
  starting transfers between devices: 0 us -> 11.9 us
  local copies, waits for them, and re-layouts: 7.33 us -> 2.71 us
  Pallas kernels: 0 us -> 3.37 us
  matrix products: 3.12 us -> 0 us
  other arithmetic: 3.3 us -> 0.68 us
  between operations: 0.82 us -> 0.09 us
    unnamed x1 -> x0, blocking collectives: 25.9 us -> none
    ppermute x0 -> x8, waiting for transfers between devices: none -> 16.5 us  [exchange(): return lax.ppermute(value, axes, pairs)]
    ppermute x0 -> x8, starting transfers between devices: none -> 11.9 us  [exchange(): return lax.ppermute(value, axes, pairs)]
    all_gather x1 -> x0, blocking collectives: 9.32 us -> none  [on_device(): blocks = lax.all_gather(own_block[None], 'tm', axis=0, tiled=True)]
    psum x1 -> x0, blocking collectives: 8.94 us -> none  [on_device(): summed = lax.psum(picked, 'space')]
    squeeze x2 -> x0, local copies, waits for them, and re-layouts: 3.72 us -> none  [on_device(): columns_both = jnp.concatenate([vecs_flat[0], vecs_flat[1]], axis=0)]
    pallas_call x0 -> x3, Pallas kernels: none -> 3.37 us  [the longest x1 1.55 us: trace(): pl.pallas_call(functools.partial(trace_kernel, orders), out_shape=jax.Sha...]
    dot_general x4 -> x0, matrix products: 3.12 us -> none  [the longest x1 1.26 us: on_device(): lax.dot_general(weights, flattened, (((1,), (1,)), ((), ())), preferred_e...]
  transfers between devices with their start and end apart: 0 -> 8, of which waited for: 0 -> 6; matrix products, arithmetic and copies ran while one was open for 0% -> 0% of each run, Pallas kernels for 0% -> 2%
where the time goes in v1:
time: 35.4 us; the launch traced here: 35.2 us
  waiting for transfers between devices  16.5 us (47%)
  starting transfers between devices  11.9 us (34%)
  Pallas kernels  3.37 us (10%)
  local copies, waits for them, and re-layouts  2.71 us (8%)
  other arithmetic  0.68 us (2%)
    ppermute x8, waiting for transfers between devices, exchange(): return lax.ppermute(value, axes, pairs)  16.5 us
    ppermute x8, starting transfers between devices, exchange(): return lax.ppermute(value, axes, pairs)  11.9 us
    unnamed x10, local copies, waits for them, and re-layouts  2.71 us
    pallas_call x1, Pallas kernels, trace(): pl.pallas_call(functools.partial(trace_kernel, orders), out_shape=jax.Sha...  1.55 us
    pallas_call x1, Pallas kernels, project(): pl.pallas_call(project_kernel, out_shape=(out, out), in_specs=[pl.BlockSp...  1 us
    pallas_call x1, Pallas kernels, mix(): pl.pallas_call(mix_kernel, out_shape=jax.ShapeDtypeStruct((momenta,) + ow...  0.81 us
  transfers between devices with their start and end apart: 8, of which 6 were waited for; matrix products, arithmetic and copies ran while one was open for 0% of the time, Pallas kernels for 2%

profile of v1, /device:TPU:0, one launch (start us, length us, event | category | flops | bytes accessed | tf_op | source)
XLA Modules:
  0.0 35.2 jit_solution(906479114548508511)
XLA Ops:
  0.0 0.0 copy-start
  0.0 0.0 copy-start.1
  0.0 1.6 %copy-done.1 = bf16[2,3,1,512,256]{4,3,2,1,0:T(8,128)(2,1)S(1)} copy-done((bf16[2,3,1,512,256]{4,3,2,1,0:T(8,128)(2,1)S(1)}, bf16[2,3,1,512,256]{4,3,2,1,0:T(8,128)(2,1)}, u32[]{:S(2)}) %copy-start.1) | copy-done | bytes 1572888
  1.6 0.0 copy-start.2
  1.6 1.1 %copy-done.2 = bf16[2,3,1,512,128]{4,3,2,1,0:T(8,128)(2,1)S(1)} copy-done((bf16[2,3,1,512,128]{4,3,2,1,0:T(8,128)(2,1)S(1)}, bf16[2,3,1,512,128]{4,3,2,1,0:T(8,128)(2,1)}, u32[]{:S(2)}) %copy-start.2) | copy-done | bytes 786456
  2.7 1.0 %project.1 = (f32[2,64,256]{2,1,0:T(8,128)S(1)}, f32[2,64,256]{2,1,0:T(8,128)S(1)}) custom-call(bf16[2,3,1,512,256]{4,3,2,1,0:T(8,128)(2,1)S(1)} %copy-done.1, bf16[2,3,1,512,128]{4,3,2,1,0:T(8,128)(2,1)S(1)} %copy-done.2), custom_call_target="tpu_custom_call" | custom-call | tf_op jit(solution)/shard_map/project/pallas_call | solution.py:49
  3.7 0.0 copy-start.3
  3.7 0.0 copy-start.4
  3.7 3.1 %collective-permute-start = (f32[2,64,256]{2,1,0:T(8,128)S(1)}, f32[2,64,256]{2,1,0:T(8,128)S(1)}, u32[]{:S(2)}, u32[]{:S(2)}) collective-permute-start(f32[2,64,256]{2,1,0:T(8,128)S(1)} %get-tuple-element.8), channel_id=1, source_target_pairs={{0,1},{1,0},{2,3},{3,2},{4,5},{5,4},{6,7},{7,6},{8,9},{9,8},{10,11... | collective-permute-start | bytes 393224 | tf_op jit(solution)/shard_map/ppermute | solution.py:166
  6.8 3.5 %collective-permute-done = f32[2,64,256]{2,1,0:T(8,128)S(1)} collective-permute-done((f32[2,64,256]{2,1,0:T(8,128)S(1)}, f32[2,64,256]{2,1,0:T(8,128)S(1)}, u32[]{:S(2)}, u32[]{:S(2)}) %collective-permute-start) | collective-permute-done | bytes 131104 | tf_op jit(solution)/shard_map/ppermute | solution.py:166
  10.3 1.7 %collective-permute-start.2 = (bf16[1,2,64,256]{3,2,1,0:T(8,128)(2,1)S(1)}, bf16[1,2,64,256]{3,2,1,0:T(8,128)(2,1)S(1)}, u32[]{:S(2)}, u32[]{:S(2)}) collective-permute-start(bf16[1,2,64,256]{3,2,1,0:T(8,128)(2,1)S(1)} %get-tuple-element.9), channel_id=1, source_target_pairs={{0,8},{1,9},{2,10},{3,11},{4,20},{5,21},{6,22},{7,23},{8,0},{9,1},... | collective-permute-start | bytes 196616 | tf_op jit(solution)/shard_map/ppermute | solution.py:166
  12.1 2.6 %collective-permute-done.2 = bf16[1,2,64,256]{3,2,1,0:T(8,128)(2,1)S(1)} collective-permute-done((bf16[1,2,64,256]{3,2,1,0:T(8,128)(2,1)S(1)}, bf16[1,2,64,256]{3,2,1,0:T(8,128)(2,1)S(1)}, u32[]{:S(2)}, u32[]{:S(2)}) %collective-permute-start.2) | collective-permute-done | bytes 65568 | tf_op jit(solution)/shard_map/ppermute | solution.py:166
  14.7 1.7 %collective-permute-start.3 = (bf16[2,2,64,256]{3,2,1,0:T(8,128)(2,1)S(1)}, bf16[2,2,64,256]{3,2,1,0:T(8,128)(2,1)S(1)}, u32[]{:S(2)}, u32[]{:S(2)}) collective-permute-start(bf16[2,2,64,256]{3,2,1,0:T(8,128)(2,1)S(1)} %pad_maximum_fusion.refs_0_), channel_id=1, source_target_pairs={{0,16},{1,17},{2,18},{3,19},{4,12},{5,13},{6,14},{7,15},{8,24},{9,... | collective-permute-start | bytes 393224 | tf_op jit(solution)/shard_map/ppermute | solution.py:166
  16.4 2.6 %collective-permute-start.1 = (f32[2,64,256]{2,1,0:T(8,128)S(1)}, f32[2,64,256]{2,1,0:T(8,128)S(1)}, u32[]{:S(2)}, u32[]{:S(2)}) collective-permute-start(f32[2,64,256]{2,1,0:T(8,128)S(1)} %get-tuple-element.10.own_ref), channel_id=1, source_target_pairs={{0,2},{1,3},{2,0},{3,1},{4,6},{5,7},{6,4},{7,5},{8,10},{9,11},{10,... | collective-permute-start | bytes 393224 | tf_op jit(solution)/shard_map/ppermute | solution.py:166
  19.0 0.0 collective-permute-start.4
  19.0 0.7 %collective-permute-done.3.refs_1_ = bf16[2,2,64,256]{3,2,1,0:T(8,128)(2,1)S(1)} collective-permute-done((bf16[2,2,64,256]{3,2,1,0:T(8,128)(2,1)S(1)}, bf16[2,2,64,256]{3,2,1,0:T(8,128)(2,1)S(1)}, u32[]{:S(2)}, u32[]{:S(2)}) %collective-permute-start.3) | collective-permute-done | bytes 131104 | tf_op jit(solution)/shard_map/ppermute | solution.py:166
  19.7 0.0 collective-permute-start.5
  19.7 4.0 %collective-permute-done.1.other_ref = f32[2,64,256]{2,1,0:T(8,128)S(1)} collective-permute-done((f32[2,64,256]{2,1,0:T(8,128)S(1)}, f32[2,64,256]{2,1,0:T(8,128)S(1)}, u32[]{:S(2)}, u32[]{:S(2)}) %collective-permute-start.1) | collective-permute-done | bytes 131104 | tf_op jit(solution)/shard_map/ppermute | solution.py:166
  23.7 0.0 copy-done
  23.7 0.8 %mix.1.mixed_ref = bf16[8,2,64,256]{3,2,1,0:T(8,128)(2,1)S(1)} custom-call(f32[2,64,256]{2,1,0:T(8,128)S(1)} %get-tuple-element.10.own_ref, f32[2,64,256]{2,1,0:T(8,128)S(1)} %collective-permute-done.1.other_ref, bf16[1,8,2,256,256]{4,3,2,1,0:T(8,128)(2,1)S(1)} %copy-done), custom_call_target="tpu_custom_call" | custom-call | flops 268435456 | bytes 262144 | tf_op jit(solution)/shard_map/mix/pallas_call | solution.py:84
  24.5 0.0 collective-permute-done.4.refs_2_
  24.5 0.0 collective-permute-done.5.refs_3_
  24.5 0.0 copy-done.3
  24.6 0.0 copy-done.4
  24.6 1.6 %trace.1 = f32[2,16,128]{2,1,0:T(8,128)S(1)} custom-call(s32[1,16]{1,0:T(1,128)S(1)} %copy-done.3, s32[1,16]{1,0:T(1,128)S(1)} %copy-done.4, bf16[8,2,64,256]{3,2,1,0:T(8,128)(2,1)S(1)} %mix.1.mixed_ref, bf16[2,2,64,256]{3,2,1,0:T(8,128)(2,1)S(1)} %pad_maximum_fusion.refs_0_, bf16[2,2,64,256]{3,2,1,0:T(8,128)(2,1)S(1)} %collective-permute-done.3.refs_1_, ...), custom_call_target="tpu_custom_call" | custom-call | tf_op jit(solution)/shard_map/trace/pallas_call | solution.py:142
  26.1 0.7 %collective-permute-start.6 = (f32[2,16,128]{2,1,0:T(8,128)S(1)}, f32[2,16,128]{2,1,0:T(8,128)S(1)}, u32[]{:S(2)}, u32[]{:S(2)}) collective-permute-start(f32[2,16,128]{2,1,0:T(8,128)S(1)} %trace.1), channel_id=1, source_target_pairs={{0,1},{1,0},{2,3},{3,2},{4,5},{5,4},{6,7},{7,6},{8,9},{9,8},{10,11... | collective-permute-start | bytes 49160 | tf_op jit(solution)/shard_map/ppermute | solution.py:166
  26.9 3.1 %collective-permute-done.6 = f32[2,16,128]{2,1,0:T(8,128)S(1)} collective-permute-done((f32[2,16,128]{2,1,0:T(8,128)S(1)}, f32[2,16,128]{2,1,0:T(8,128)S(1)}, u32[]{:S(2)}, u32[]{:S(2)}) %collective-permute-start.6) | collective-permute-done | bytes 16416 | tf_op jit(solution)/shard_map/ppermute | solution.py:166
  29.9 2.0 %collective-permute-start.7 = (f32[2,16,128]{2,1,0:T(8,128)S(1)}, f32[2,16,128]{2,1,0:T(8,128)S(1)}, u32[]{:S(2)}, u32[]{:S(2)}) collective-permute-start(f32[2,16,128]{2,1,0:T(8,128)S(1)} %add.10), channel_id=1, source_target_pairs={{0,2},{1,3},{2,0},{3,1},{4,6},{5,7},{6,4},{7,5},{8,10},{9,11},{10,... | collective-permute-start | bytes 49160 | tf_op jit(solution)/shard_map/ppermute | solution.py:166
  32.0 2.6 %collective-permute-done.7 = f32[2,16,128]{2,1,0:T(8,128)S(1)} collective-permute-done((f32[2,16,128]{2,1,0:T(8,128)S(1)}, f32[2,16,128]{2,1,0:T(8,128)S(1)}, u32[]{:S(2)}, u32[]{:S(2)}) %collective-permute-start.7) | collective-permute-done | bytes 16416 | tf_op jit(solution)/shard_map/ppermute | solution.py:166
  34.6 0.6 %add_reduce_fusion = f32[2,16]{1,0:T(2,128)} fusion(f32[2,16,128]{2,1,0:T(8,128)S(1)} %add.10, f32[2,16,128]{2,1,0:T(8,128)S(1)} %collective-permute-done.7), kind=kLoop, calls=%fused_computation.2 | loop fusion | flops 8160 | bytes 32896 | tf_op jit(solution)/shard_map/reduce_sum | solution.py:189
  (3 shorter events, 0.0 us)
Async XLA Ops:
  0.0 23.7 %copy-start = (bf16[1,8,2,256,256]{4,3,2,1,0:T(8,128)(2,1)S(1)}, bf16[1,8,2,256,256]{4,3,2,1,0:T(8,128)(2,1)}, u32[]{:S(2)}) copy-start(bf16[1,8,2,256,256]{4,3,2,1,0:T(8,128)(2,1)} %elem_ref.1) | copy-start | bytes 6291460
  0.0 1.6 %copy-start.1 = (bf16[2,3,1,512,256]{4,3,2,1,0:T(8,128)(2,1)S(1)}, bf16[2,3,1,512,256]{4,3,2,1,0:T(8,128)(2,1)}, u32[]{:S(2)}) copy-start(bf16[2,3,1,512,256]{4,3,2,1,0:T(8,128)(2,1)} %vec_hbm.1) | copy-start | bytes 4718596
  1.6 1.1 %copy-start.2 = (bf16[2,3,1,512,128]{4,3,2,1,0:T(8,128)(2,1)S(1)}, bf16[2,3,1,512,128]{4,3,2,1,0:T(8,128)(2,1)}, u32[]{:S(2)}) copy-start(bf16[2,3,1,512,128]{4,3,2,1,0:T(8,128)(2,1)} %prop_hbm.1) | copy-start | bytes 2359300
  3.7 20.8 %copy-start.3 = (s32[1,16]{1,0:T(1,128)S(1)}, s32[1,16]{1,0:T(1,128)}, u32[]{:S(2)}) copy-start(s32[1,16]{1,0:T(1,128)} %sink_ref.1) | copy-start | bytes 196
  3.7 20.8 %copy-start.4 = (s32[1,16]{1,0:T(1,128)S(1)}, s32[1,16]{1,0:T(1,128)}, u32[]{:S(2)}) copy-start(s32[1,16]{1,0:T(1,128)} %mom_ref.1) | copy-start | bytes 196
  3.7 6.6 %collective-permute-start = (f32[2,64,256]{2,1,0:T(8,128)S(1)}, f32[2,64,256]{2,1,0:T(8,128)S(1)}, u32[]{:S(2)}, u32[]{:S(2)}) collective-permute-start(f32[2,64,256]{2,1,0:T(8,128)S(1)} %get-tuple-element.8), channel_id=1, source_target_pairs={{0,1},{1,0},{2,3},{3,2},{4,5},{5,4},{6,7},{7,6},{8,9},{9,8},{10,11... | collective-permute-start | bytes 393224 | tf_op jit(solution)/shard_map/ppermute | solution.py:166
  10.3 4.3 %collective-permute-start.2 = (bf16[1,2,64,256]{3,2,1,0:T(8,128)(2,1)S(1)}, bf16[1,2,64,256]{3,2,1,0:T(8,128)(2,1)S(1)}, u32[]{:S(2)}, u32[]{:S(2)}) collective-permute-start(bf16[1,2,64,256]{3,2,1,0:T(8,128)(2,1)S(1)} %get-tuple-element.9), channel_id=1, source_target_pairs={{0,8},{1,9},{2,10},{3,11},{4,20},{5,21},{6,22},{7,23},{8,0},{9,1},... | collective-permute-start | bytes 196616 | tf_op jit(solution)/shard_map/ppermute | solution.py:166
  14.7 5.0 %collective-permute-start.3 = (bf16[2,2,64,256]{3,2,1,0:T(8,128)(2,1)S(1)}, bf16[2,2,64,256]{3,2,1,0:T(8,128)(2,1)S(1)}, u32[]{:S(2)}, u32[]{:S(2)}) collective-permute-start(bf16[2,2,64,256]{3,2,1,0:T(8,128)(2,1)S(1)} %pad_maximum_fusion.refs_0_), channel_id=1, source_target_pairs={{0,16},{1,17},{2,18},{3,19},{4,12},{5,13},{6,14},{7,15},{8,24},{9,... | collective-permute-start | bytes 393224 | tf_op jit(solution)/shard_map/ppermute | solution.py:166
  16.4 7.3 %collective-permute-start.1 = (f32[2,64,256]{2,1,0:T(8,128)S(1)}, f32[2,64,256]{2,1,0:T(8,128)S(1)}, u32[]{:S(2)}, u32[]{:S(2)}) collective-permute-start(f32[2,64,256]{2,1,0:T(8,128)S(1)} %get-tuple-element.10.own_ref), channel_id=1, source_target_pairs={{0,2},{1,3},{2,0},{3,1},{4,6},{5,7},{6,4},{7,5},{8,10},{9,11},{10,... | collective-permute-start | bytes 393224 | tf_op jit(solution)/shard_map/ppermute | solution.py:166
  19.0 5.5 %collective-permute-start.4 = (bf16[2,2,64,256]{3,2,1,0:T(8,128)(2,1)S(1)}, bf16[2,2,64,256]{3,2,1,0:T(8,128)(2,1)S(1)}, u32[]{:S(2)}, u32[]{:S(2)}) collective-permute-start(bf16[2,2,64,256]{3,2,1,0:T(8,128)(2,1)S(1)} %pad_maximum_fusion.refs_0_), channel_id=1, source_target_pairs={{0,4},{1,5},{2,6},{3,7},{4,0},{5,1},{6,2},{7,3},{8,12},{9,13},{10,... | collective-permute-start | bytes 393224 | tf_op jit(solution)/shard_map/ppermute | solution.py:166
  19.7 4.8 %collective-permute-start.5 = (bf16[2,2,64,256]{3,2,1,0:T(8,128)(2,1)S(1)}, bf16[2,2,64,256]{3,2,1,0:T(8,128)(2,1)S(1)}, u32[]{:S(2)}, u32[]{:S(2)}) collective-permute-start(bf16[2,2,64,256]{3,2,1,0:T(8,128)(2,1)S(1)} %collective-permute-done.3.refs_1_), channel_id=1, source_target_pairs={{0,4},{1,5},{2,6},{3,7},{4,0},{5,1},{6,2},{7,3},{8,12},{9,13},{10,... | collective-permute-start | bytes 393224 | tf_op jit(solution)/shard_map/ppermute | solution.py:166
  26.1 3.8 %collective-permute-start.6 = (f32[2,16,128]{2,1,0:T(8,128)S(1)}, f32[2,16,128]{2,1,0:T(8,128)S(1)}, u32[]{:S(2)}, u32[]{:S(2)}) collective-permute-start(f32[2,16,128]{2,1,0:T(8,128)S(1)} %trace.1), channel_id=1, source_target_pairs={{0,1},{1,0},{2,3},{3,2},{4,5},{5,4},{6,7},{7,6},{8,9},{9,8},{10,11... | collective-permute-start | bytes 49160 | tf_op jit(solution)/shard_map/ppermute | solution.py:166
  29.9 4.6 %collective-permute-start.7 = (f32[2,16,128]{2,1,0:T(8,128)S(1)}, f32[2,16,128]{2,1,0:T(8,128)S(1)}, u32[]{:S(2)}, u32[]{:S(2)}) collective-permute-start(f32[2,16,128]{2,1,0:T(8,128)S(1)} %add.10), channel_id=1, source_target_pairs={{0,2},{1,3},{2,0},{3,1},{4,6},{5,7},{6,4},{7,5},{8,10},{9,11},{10,... | collective-permute-start | bytes 49160 | tf_op jit(solution)/shard_map/ppermute | solution.py:166

commit v2 on v1

--- a/solution.py
+++ b/solution.py
@@ -57,9 +57,13 @@
             pltpu.VMEM((2 * columns, 2 * vec_count), jnp.float32),
             pltpu.SemaphoreType.DMA((2, colours)),
         ],
-        compiler_params=pltpu.CompilerParams(vmem_limit_bytes=16 * MIB),
+        compiler_params=pltpu.CompilerParams(vmem_limit_bytes=53 * MIB),
         name="project",
     )(eigvecs, propagator)
+
+
+def rounded(value):
+    return value.astype(jnp.bfloat16).astype(jnp.float32)
 
 
 def mix_kernel(own_ref, other_ref, elem_ref, mixed_ref):
@@ -74,8 +78,8 @@
             )
             for r in range(2)
         )
-        mixed_ref[p, 0] = (by_real[:half] - by_imag[half:]).astype(jnp.bfloat16)
-        mixed_ref[p, 1] = (by_imag[:half] + by_real[half:]).astype(jnp.bfloat16)
+        mixed_ref[p, 0] = rounded(by_real[:half] - by_imag[half:])
+        mixed_ref[p, 1] = rounded(by_imag[:half] + by_real[half:])
 
 
 def mix(own, other, elementals):
@@ -83,7 +87,7 @@
     size = own.size
     return pl.pallas_call(
         mix_kernel,
-        out_shape=jax.ShapeDtypeStruct((momenta,) + own.shape, jnp.bfloat16),
+        out_shape=jax.ShapeDtypeStruct((momenta,) + own.shape, jnp.float32),
         in_specs=[pl.BlockSpec(memory_space=pltpu.VMEM)] * 3,
         out_specs=pl.BlockSpec(memory_space=pltpu.VMEM),
         compiler_params=pltpu.CompilerParams(vmem_limit_bytes=16 * MIB),
@@ -95,57 +99,51 @@
 
 
 def trace_kernel(orders, sink_ref, mom_ref, mixed_ref, *refs):
-    groups, out_ref, sums_ref = refs[:-2], refs[-2], refs[-1]
+    groups, out_ref, slices_ref, sums_ref = refs[:-3], refs[-3], refs[-2], refs[-1]
     items = out_ref.shape[1]
+    per_group = groups[0].shape[0]
     own_slice = lax.axis_index("tm")
     own_core = own_slice & 1
-
-    def one(k, carry):
+    for g, ref in enumerate(groups):
+        slices_ref[g * per_group : (g + 1) * per_group] = ref[...]
+    for k in range(items):
         p = mom_ref[0, k]
         away = sink_ref[0, k] ^ own_slice
         crossed = away & 1
-        holder = own_core ^ crossed
         slots = []
         for order in orders:
             slot = 0
             for place, bit in enumerate(order):
                 slot = slot + (((away >> bit) & 1) << place)
             slots.append(slot)
-        slot = jnp.where(holder == 0, slots[0], slots[1])
-        late = slot >> (len(orders[0]) - 1)
-        inner = slot & ((1 << (len(orders[0]) - 1)) - 1)
-        group = crossed * 2 + late
-        mixed_real = mixed_ref[p, 0].astype(jnp.float32)
-        mixed_imag = mixed_ref[p, 1].astype(jnp.float32)
-        for g, ref in enumerate(groups):
-
-            @pl.when(group == g)
-            def _(ref=ref):
-                real = ref[inner, 0].astype(jnp.float32)
-                imag = ref[inner, 1].astype(jnp.float32)
-                for o, value in enumerate(
-                    (mixed_real * real + mixed_imag * imag, mixed_imag * real - mixed_real * imag)
-                ):
-                    rows, lanes = value.shape
-                    value = jnp.sum(value.reshape(rows // 8, 8, lanes), axis=0)
-                    value = sum(value[:, i * 128 : (i + 1) * 128] for i in range(lanes // 128))
-                    sums_ref[o, k] = value
-
-        return carry
-
-    lax.fori_loop(0, items, one, 0)
+        slot = jnp.where(own_core ^ crossed == 0, slots[0], slots[1])
+        slot = slot + crossed * (2 * per_group)
+        real = slices_ref[slot, 0].astype(jnp.float32)
+        imag = slices_ref[slot, 1].astype(jnp.float32)
+        mixed_real = mixed_ref[p, 0]
+        mixed_imag = mixed_ref[p, 1]
+        for o, value in enumerate(
+            (mixed_real * real + mixed_imag * imag, mixed_imag * real - mixed_real * imag)
+        ):
+            rows, lanes = value.shape
+            value = jnp.sum(value.reshape(rows // 8, 8, lanes), axis=0)
+            sums_ref[o, k] = sum(value[:, i * 128 : (i + 1) * 128] for i in range(lanes // 128))
     out_ref[...] = jnp.sum(sums_ref[...], axis=2)
 
 
 def trace(orders, sink_times, momenta, mixed, groups):
     items = sink_times.shape[1]
+    per_group = groups[0].shape[0]
     return pl.pallas_call(
         functools.partial(trace_kernel, orders),
         out_shape=jax.ShapeDtypeStruct((2, items, 128), jnp.float32),
         in_specs=[pl.BlockSpec(memory_space=pltpu.SMEM)] * 2
         + [pl.BlockSpec(memory_space=pltpu.VMEM)] * (1 + len(groups)),
         out_specs=pl.BlockSpec(memory_space=pltpu.VMEM),
-        scratch_shapes=[pltpu.VMEM((2, items, 8, 128), jnp.float32)],
+        scratch_shapes=[
+            pltpu.VMEM((len(groups) * per_group,) + groups[0].shape[1:], jnp.bfloat16),
+            pltpu.VMEM((2, items, 8, 128), jnp.float32),
+        ],
         compiler_params=pltpu.CompilerParams(vmem_limit_bytes=16 * MIB),
         name="trace",
     )(sink_times, momenta, mixed, *groups)
@@ -180,6 +178,7 @@
         arrived = exchange(blocks, lambda t, s: (t ^ (1 << orders[t & 1][step]), s))
         if step < slice_bits - 2:
             blocks = jnp.concatenate([blocks, arrived], axis=0)
+    arrived, other = lax.optimization_barrier((arrived, other))
     cross = lambda t, s: (t ^ 1, s)
     groups = [blocks, arrived, exchange(blocks, cross), exchange(arrived, cross)]
     mixed = mix(total, other, elementals)

time: 35.4 us -> 30 us (0.85)
  waiting for transfers between devices: 16.5 us -> 11.7 us
  local copies, waits for them, and re-layouts: 2.71 us -> 0.02 us
  starting transfers between devices: 11.9 us -> 13.4 us
  Pallas kernels: 3.37 us -> 3.99 us
    ppermute x8, waiting for transfers between devices: 16.5 us -> 11.7 us  [exchange(): return lax.ppermute(value, axes, pairs)]
    unnamed x10 -> x6, local copies, waits for them, and re-layouts: 2.71 us -> 0.02 us
    ppermute x8, starting transfers between devices: 11.9 us -> 13.4 us  [exchange(): return lax.ppermute(value, axes, pairs)]
    pallas_call x1, Pallas kernels: 1 us -> 2.16 us  [project(): pl.pallas_call(project_kernel, out_shape=(out, out), in_specs=[pl.BlockSp...]
    pallas_call x1, Pallas kernels: 1.55 us -> 1.02 us  [trace(): pl.pallas_call(functools.partial(trace_kernel, orders), out_shape=jax.Sha...]
  transfers between devices with their start and end apart: 8 -> 8, of which waited for: 6 -> 5; matrix products, arithmetic and copies ran while one was open for 0% -> 0% of each run, Pallas kernels for 2% -> 3%
where the time goes in v2:
time: 30 us; the launch traced here: 29.8 us
  starting transfers between devices  13.4 us (45%)
  waiting for transfers between devices  11.7 us (39%)
  Pallas kernels  3.99 us (13%)
  other arithmetic  0.69 us (2%)
    ppermute x8, starting transfers between devices, exchange(): return lax.ppermute(value, axes, pairs)  13.4 us
    ppermute x8, waiting for transfers between devices, exchange(): return lax.ppermute(value, axes, pairs)  11.7 us
    pallas_call x1, Pallas kernels, project(): pl.pallas_call(project_kernel, out_shape=(out, out), in_specs=[pl.BlockSp...  2.16 us
    pallas_call x1, Pallas kernels, trace(): pl.pallas_call(functools.partial(trace_kernel, orders), out_shape=jax.Sha...  1.02 us
    pallas_call x1, Pallas kernels, mix(): pl.pallas_call(mix_kernel, out_shape=jax.ShapeDtypeStruct((momenta,) + ow...  0.82 us
    reduce_sum x1, other arithmetic, by_exchanges(): return jnp.sum(partial, axis=-1)[:, None, :]  0.65 us
  transfers between devices with their start and end apart: 8, of which 5 were waited for; matrix products, arithmetic and copies ran while one was open for 0% of the time, Pallas kernels for 3%

profile of v2, /device:TPU:0, one launch (start us, length us, event | category | flops | bytes accessed | tf_op | source)
XLA Modules:
  0.0 29.8 jit_solution(3168905682755991057)
XLA Ops:
  0.0 0.0 copy-start
  0.0 2.2 %project.1 = (f32[2,64,256]{2,1,0:T(8,128)S(1)}, f32[2,64,256]{2,1,0:T(8,128)S(1)}) custom-call(bf16[2,3,1,512,256]{4,3,2,1,0:T(8,128)(2,1)} %vec_hbm.1, bf16[2,3,1,512,128]{4,3,2,1,0:T(8,128)(2,1)} %prop_hbm.1), custom_call_target="tpu_custom_call" | custom-call | tf_op jit(solution)/shard_map/project/pallas_call | solution.py:49
  2.2 0.0 copy-start.1
  2.2 0.0 copy-start.2
  2.2 3.1 %collective-permute-start = (f32[2,64,256]{2,1,0:T(8,128)S(1)}, f32[2,64,256]{2,1,0:T(8,128)S(1)}, u32[]{:S(2)}, u32[]{:S(2)}) collective-permute-start(f32[2,64,256]{2,1,0:T(8,128)S(1)} %get-tuple-element.10), channel_id=1, source_target_pairs={{0,1},{1,0},{2,3},{3,2},{4,5},{5,4},{6,7},{7,6},{8,9},{9,8},{10,11... | collective-permute-start | bytes 393224 | tf_op jit(solution)/shard_map/ppermute | solution.py:164
  5.3 3.5 %collective-permute-done = f32[2,64,256]{2,1,0:T(8,128)S(1)} collective-permute-done((f32[2,64,256]{2,1,0:T(8,128)S(1)}, f32[2,64,256]{2,1,0:T(8,128)S(1)}, u32[]{:S(2)}, u32[]{:S(2)}) %collective-permute-start) | collective-permute-done | bytes 131104 | tf_op jit(solution)/shard_map/ppermute | solution.py:164
  8.8 1.7 %collective-permute-start.1 = (bf16[1,2,64,256]{3,2,1,0:T(8,128)(2,1)S(1)}, bf16[1,2,64,256]{3,2,1,0:T(8,128)(2,1)S(1)}, u32[]{:S(2)}, u32[]{:S(2)}) collective-permute-start(bf16[1,2,64,256]{3,2,1,0:T(8,128)(2,1)S(1)} %get-tuple-element.13), channel_id=1, source_target_pairs={{0,8},{1,9},{2,10},{3,11},{4,20},{5,21},{6,22},{7,23},{8,0},{9,1},... | collective-permute-start | bytes 196616 | tf_op jit(solution)/shard_map/ppermute | solution.py:164
  10.5 2.6 %collective-permute-start.3 = (f32[2,64,256]{2,1,0:T(8,128)S(1)}, f32[2,64,256]{2,1,0:T(8,128)S(1)}, u32[]{:S(2)}, u32[]{:S(2)}) collective-permute-start(f32[2,64,256]{2,1,0:T(8,128)S(1)} %get-tuple-element.14.own_ref), channel_id=1, source_target_pairs={{0,2},{1,3},{2,0},{3,1},{4,6},{5,7},{6,4},{7,5},{8,10},{9,11},{10,... | collective-permute-start | bytes 393224 | tf_op jit(solution)/shard_map/ppermute | solution.py:164
  13.1 0.0 collective-permute-done.1
  13.2 1.7 %collective-permute-start.2 = (bf16[2,2,64,256]{3,2,1,0:T(8,128)(2,1)S(1)}, bf16[2,2,64,256]{3,2,1,0:T(8,128)(2,1)S(1)}, u32[]{:S(2)}, u32[]{:S(2)}) collective-permute-start(bf16[2,2,64,256]{3,2,1,0:T(8,128)(2,1)S(1)} %pad_maximum_fusion.refs_0_), channel_id=1, source_target_pairs={{0,16},{1,17},{2,18},{3,19},{4,12},{5,13},{6,14},{7,15},{8,24},{9,... | collective-permute-start | bytes 393224 | tf_op jit(solution)/shard_map/ppermute | solution.py:164
  14.9 0.0 collective-permute-start.4
  14.9 3.4 %collective-permute-done.3.other_ref = f32[2,64,256]{2,1,0:T(8,128)S(1)} collective-permute-done((f32[2,64,256]{2,1,0:T(8,128)S(1)}, f32[2,64,256]{2,1,0:T(8,128)S(1)}, u32[]{:S(2)}, u32[]{:S(2)}) %collective-permute-start.3) | collective-permute-done | bytes 131104 | tf_op jit(solution)/shard_map/ppermute | solution.py:164
  18.3 0.0 collective-permute-done.2.refs_1_
  18.3 0.0 collective-permute-start.5
  18.4 0.0 copy-done
  18.4 0.8 %mix.1.mixed_ref = f32[8,2,64,256]{3,2,1,0:T(8,128)S(1)} custom-call(f32[2,64,256]{2,1,0:T(8,128)S(1)} %get-tuple-element.14.own_ref, f32[2,64,256]{2,1,0:T(8,128)S(1)} %collective-permute-done.3.other_ref, bf16[1,8,2,256,256]{4,3,2,1,0:T(8,128)(2,1)S(1)} %copy-done), custom_call_target="tpu_custom_call" | custom-call | flops 268435456 | bytes 262144 | tf_op jit(solution)/shard_map/mix/pallas_call | solution.py:88
  19.2 0.0 collective-permute-done.4.refs_2_
  19.2 0.5 %collective-permute-done.5.refs_3_ = bf16[2,2,64,256]{3,2,1,0:T(8,128)(2,1)S(1)} collective-permute-done((bf16[2,2,64,256]{3,2,1,0:T(8,128)(2,1)S(1)}, bf16[2,2,64,256]{3,2,1,0:T(8,128)(2,1)S(1)}, u32[]{:S(2)}, u32[]{:S(2)}) %collective-permute-start.5) | collective-permute-done | bytes 131104 | tf_op jit(solution)/shard_map/ppermute | solution.py:164
  19.7 0.0 copy-done.1
  19.7 0.0 copy-done.2
  19.7 1.0 %trace.1 = f32[2,16,128]{2,1,0:T(8,128)S(1)} custom-call(s32[1,16]{1,0:T(1,128)S(1)} %copy-done.1, s32[1,16]{1,0:T(1,128)S(1)} %copy-done.2, f32[8,2,64,256]{3,2,1,0:T(8,128)S(1)} %mix.1.mixed_ref, bf16[2,2,64,256]{3,2,1,0:T(8,128)(2,1)S(1)} %pad_maximum_fusion.refs_0_, bf16[2,2,64,256]{3,2,1,0:T(8,128)(2,1)S(1)} %collective-permute-done.2.refs_1_, ...), custom_call_target="tpu_custom_call" | custom-call | tf_op jit(solution)/shard_map/trace/pallas_call | solution.py:137
  20.7 1.6 %collective-permute-start.6 = (f32[2,16,128]{2,1,0:T(8,128)S(1)}, f32[2,16,128]{2,1,0:T(8,128)S(1)}, u32[]{:S(2)}, u32[]{:S(2)}) collective-permute-start(f32[2,16,128]{2,1,0:T(8,128)S(1)} %trace.1), channel_id=1, source_target_pairs={{0,1},{1,0},{2,3},{3,2},{4,5},{5,4},{6,7},{7,6},{8,9},{9,8},{10,11... | collective-permute-start | bytes 49160 | tf_op jit(solution)/shard_map/ppermute | solution.py:164
  22.4 2.2 %collective-permute-done.6 = f32[2,16,128]{2,1,0:T(8,128)S(1)} collective-permute-done((f32[2,16,128]{2,1,0:T(8,128)S(1)}, f32[2,16,128]{2,1,0:T(8,128)S(1)}, u32[]{:S(2)}, u32[]{:S(2)}) %collective-permute-start.6) | collective-permute-done | bytes 16416 | tf_op jit(solution)/shard_map/ppermute | solution.py:164
  24.5 2.6 %collective-permute-start.7 = (f32[2,16,128]{2,1,0:T(8,128)S(1)}, f32[2,16,128]{2,1,0:T(8,128)S(1)}, u32[]{:S(2)}, u32[]{:S(2)}) collective-permute-start(f32[2,16,128]{2,1,0:T(8,128)S(1)} %add.10), channel_id=1, source_target_pairs={{0,2},{1,3},{2,0},{3,1},{4,6},{5,7},{6,4},{7,5},{8,10},{9,11},{10,... | collective-permute-start | bytes 49160 | tf_op jit(solution)/shard_map/ppermute | solution.py:164
  27.1 2.0 %collective-permute-done.7 = f32[2,16,128]{2,1,0:T(8,128)S(1)} collective-permute-done((f32[2,16,128]{2,1,0:T(8,128)S(1)}, f32[2,16,128]{2,1,0:T(8,128)S(1)}, u32[]{:S(2)}, u32[]{:S(2)}) %collective-permute-start.7) | collective-permute-done | bytes 16416 | tf_op jit(solution)/shard_map/ppermute | solution.py:164
  29.2 0.6 %add_reduce_fusion = f32[2,16]{1,0:T(2,128)} fusion(f32[2,16,128]{2,1,0:T(8,128)S(1)} %add.10, f32[2,16,128]{2,1,0:T(8,128)S(1)} %collective-permute-done.7), kind=kLoop, calls=%fused_computation.2 | loop fusion | flops 8160 | bytes 32896 | tf_op jit(solution)/shard_map/reduce_sum | solution.py:188
  (3 shorter events, 0.0 us)
Async XLA Ops:
  0.0 18.4 %copy-start = (bf16[1,8,2,256,256]{4,3,2,1,0:T(8,128)(2,1)S(1)}, bf16[1,8,2,256,256]{4,3,2,1,0:T(8,128)(2,1)}, u32[]{:S(2)}) copy-start(bf16[1,8,2,256,256]{4,3,2,1,0:T(8,128)(2,1)} %elem_ref.1) | copy-start | bytes 6291460
  2.2 17.5 %copy-start.1 = (s32[1,16]{1,0:T(1,128)S(1)}, s32[1,16]{1,0:T(1,128)}, u32[]{:S(2)}) copy-start(s32[1,16]{1,0:T(1,128)} %sink_ref.1) | copy-start | bytes 196
  2.2 17.5 %copy-start.2 = (s32[1,16]{1,0:T(1,128)S(1)}, s32[1,16]{1,0:T(1,128)}, u32[]{:S(2)}) copy-start(s32[1,16]{1,0:T(1,128)} %mom_ref.1) | copy-start | bytes 196
  2.2 6.6 %collective-permute-start = (f32[2,64,256]{2,1,0:T(8,128)S(1)}, f32[2,64,256]{2,1,0:T(8,128)S(1)}, u32[]{:S(2)}, u32[]{:S(2)}) collective-permute-start(f32[2,64,256]{2,1,0:T(8,128)S(1)} %get-tuple-element.10), channel_id=1, source_target_pairs={{0,1},{1,0},{2,3},{3,2},{4,5},{5,4},{6,7},{7,6},{8,9},{9,8},{10,11... | collective-permute-start | bytes 393224 | tf_op jit(solution)/shard_map/ppermute | solution.py:164
  8.8 4.3 %collective-permute-start.1 = (bf16[1,2,64,256]{3,2,1,0:T(8,128)(2,1)S(1)}, bf16[1,2,64,256]{3,2,1,0:T(8,128)(2,1)S(1)}, u32[]{:S(2)}, u32[]{:S(2)}) collective-permute-start(bf16[1,2,64,256]{3,2,1,0:T(8,128)(2,1)S(1)} %get-tuple-element.13), channel_id=1, source_target_pairs={{0,8},{1,9},{2,10},{3,11},{4,20},{5,21},{6,22},{7,23},{8,0},{9,1},... | collective-permute-start | bytes 196616 | tf_op jit(solution)/shard_map/ppermute | solution.py:164
  10.5 7.8 %collective-permute-start.3 = (f32[2,64,256]{2,1,0:T(8,128)S(1)}, f32[2,64,256]{2,1,0:T(8,128)S(1)}, u32[]{:S(2)}, u32[]{:S(2)}) collective-permute-start(f32[2,64,256]{2,1,0:T(8,128)S(1)} %get-tuple-element.14.own_ref), channel_id=1, source_target_pairs={{0,2},{1,3},{2,0},{3,1},{4,6},{5,7},{6,4},{7,5},{8,10},{9,11},{10,... | collective-permute-start | bytes 393224 | tf_op jit(solution)/shard_map/ppermute | solution.py:164
  13.2 5.2 %collective-permute-start.2 = (bf16[2,2,64,256]{3,2,1,0:T(8,128)(2,1)S(1)}, bf16[2,2,64,256]{3,2,1,0:T(8,128)(2,1)S(1)}, u32[]{:S(2)}, u32[]{:S(2)}) collective-permute-start(bf16[2,2,64,256]{3,2,1,0:T(8,128)(2,1)S(1)} %pad_maximum_fusion.refs_0_), channel_id=1, source_target_pairs={{0,16},{1,17},{2,18},{3,19},{4,12},{5,13},{6,14},{7,15},{8,24},{9,... | collective-permute-start | bytes 393224 | tf_op jit(solution)/shard_map/ppermute | solution.py:164
  14.9 4.3 %collective-permute-start.4 = (bf16[2,2,64,256]{3,2,1,0:T(8,128)(2,1)S(1)}, bf16[2,2,64,256]{3,2,1,0:T(8,128)(2,1)S(1)}, u32[]{:S(2)}, u32[]{:S(2)}) collective-permute-start(bf16[2,2,64,256]{3,2,1,0:T(8,128)(2,1)S(1)} %pad_maximum_fusion.refs_0_), channel_id=1, source_target_pairs={{0,4},{1,5},{2,6},{3,7},{4,0},{5,1},{6,2},{7,3},{8,12},{9,13},{10,... | collective-permute-start | bytes 393224 | tf_op jit(solution)/shard_map/ppermute | solution.py:164
  18.3 1.3 %collective-permute-start.5 = (bf16[2,2,64,256]{3,2,1,0:T(8,128)(2,1)S(1)}, bf16[2,2,64,256]{3,2,1,0:T(8,128)(2,1)S(1)}, u32[]{:S(2)}, u32[]{:S(2)}) collective-permute-start(bf16[2,2,64,256]{3,2,1,0:T(8,128)(2,1)S(1)} %collective-permute-done.2.refs_1_), channel_id=1, source_target_pairs={{0,4},{1,5},{2,6},{3,7},{4,0},{5,1},{6,2},{7,3},{8,12},{9,13},{10,... | collective-permute-start | bytes 393224 | tf_op jit(solution)/shard_map/ppermute | solution.py:164
  20.7 3.8 %collective-permute-start.6 = (f32[2,16,128]{2,1,0:T(8,128)S(1)}, f32[2,16,128]{2,1,0:T(8,128)S(1)}, u32[]{:S(2)}, u32[]{:S(2)}) collective-permute-start(f32[2,16,128]{2,1,0:T(8,128)S(1)} %trace.1), channel_id=1, source_target_pairs={{0,1},{1,0},{2,3},{3,2},{4,5},{5,4},{6,7},{7,6},{8,9},{9,8},{10,11... | collective-permute-start | bytes 49160 | tf_op jit(solution)/shard_map/ppermute | solution.py:164
  24.5 4.6 %collective-permute-start.7 = (f32[2,16,128]{2,1,0:T(8,128)S(1)}, f32[2,16,128]{2,1,0:T(8,128)S(1)}, u32[]{:S(2)}, u32[]{:S(2)}) collective-permute-start(f32[2,16,128]{2,1,0:T(8,128)S(1)} %add.10), channel_id=1, source_target_pairs={{0,2},{1,3},{2,0},{3,1},{4,6},{5,7},{6,4},{7,5},{8,10},{9,11},{10,... | collective-permute-start | bytes 49160 | tf_op jit(solution)/shard_map/ppermute | solution.py:164

commit v3 on v2

--- a/solution.py
+++ b/solution.py
@@ -117,6 +117,7 @@
                 slot = slot + (((away >> bit) & 1) << place)
             slots.append(slot)
         slot = jnp.where(own_core ^ crossed == 0, slots[0], slots[1])
+        crossed = crossed ^ (slot >> (len(orders[0]) - 1))
         slot = slot + crossed * (2 * per_group)
         real = slices_ref[slot, 0].astype(jnp.float32)
         imag = slices_ref[slot, 1].astype(jnp.float32)
@@ -175,7 +176,8 @@
             total = total + other
         other = across(total, bit)
     for step in range(slice_bits - 1):
-        arrived = exchange(blocks, lambda t, s: (t ^ (1 << orders[t & 1][step]), s))
+        flip = 1 if step == slice_bits - 2 else 0
+        arrived = exchange(blocks, lambda t, s: (t ^ (1 << orders[t & 1][step]) ^ flip, s))
         if step < slice_bits - 2:
             blocks = jnp.concatenate([blocks, arrived], axis=0)
     arrived, other = lax.optimization_barrier((arrived, other))
@@ -184,7 +186,8 @@
     mixed = mix(total, other, elementals)
     partial = trace(orders, sink_times, momenta, mixed, groups)
     for bit in range(space_bits):
-        partial = partial + across(partial, bit)
+        far = exchange(partial, lambda t, s: (t ^ 1, s ^ (1 << bit)))
+        partial = far + exchange(partial, cross)
     return jnp.sum(partial, axis=-1)[:, None, :]
 
 
@@ -232,15 +235,12 @@
     return summed[:, None, :]
 
 
-def power_of_two(count):
-    return count & (count - 1) == 0
-
-
 def solution(mesh):
     slice_count, space_count = mesh.shape["tm"], mesh.shape["space"]
+    slice_bits, space_bits = slice_count.bit_length() - 1, space_count.bit_length() - 1
     on_device = by_collectives
-    if power_of_two(slice_count) and power_of_two(space_count):
-        if slice_count > 4 and space_count > 2:
+    if (slice_count, space_count) == (1 << slice_bits, 1 << space_bits):
+        if slice_bits > 2 and space_bits > 0 and space_bits % 2 == 0:
             on_device = functools.partial(by_exchanges, slice_count, space_count)
     return jax.shard_map(
         on_device,

time: 30 us -> 28.9 us (0.963)
  starting transfers between devices: 13.4 us -> 12.6 us
  waiting for transfers between devices: 11.7 us -> 11.3 us
    ppermute x8 -> x10, starting transfers between devices: 13.4 us -> 12.6 us  [exchange(): return lax.ppermute(value, axes, pairs)]
    ppermute x8 -> x10, waiting for transfers between devices: 11.7 us -> 11.3 us  [exchange(): return lax.ppermute(value, axes, pairs)]
  transfers between devices with their start and end apart: 8 -> 10, of which waited for: 5 -> 5; matrix products, arithmetic and copies ran while one was open for 0% -> 0% of each run, Pallas kernels for 3% -> 3%
where the time goes in v3:
time: 28.9 us; the launch traced here: 28.7 us
  starting transfers between devices  12.6 us (44%)
  waiting for transfers between devices  11.3 us (39%)
  Pallas kernels  3.96 us (14%)
  other arithmetic  0.69 us (2%)
    ppermute x10, starting transfers between devices, exchange(): return lax.ppermute(value, axes, pairs)  12.6 us
    ppermute x10, waiting for transfers between devices, exchange(): return lax.ppermute(value, axes, pairs)  11.3 us
    pallas_call x1, Pallas kernels, project(): pl.pallas_call(project_kernel, out_shape=(out, out), in_specs=[pl.BlockSp...  2.16 us
    pallas_call x1, Pallas kernels, trace(): pl.pallas_call(functools.partial(trace_kernel, orders), out_shape=jax.Sha...  0.98 us
    pallas_call x1, Pallas kernels, mix(): pl.pallas_call(mix_kernel, out_shape=jax.ShapeDtypeStruct((momenta,) + ow...  0.82 us
    reduce_sum x1, other arithmetic, by_exchanges(): return jnp.sum(partial, axis=-1)[:, None, :]  0.65 us
  transfers between devices with their start and end apart: 10, of which 5 were waited for; matrix products, arithmetic and copies ran while one was open for 0% of the time, Pallas kernels for 3%

profile of v3, /device:TPU:0, one launch (start us, length us, event | category | flops | bytes accessed | tf_op | source)
XLA Modules:
  0.0 28.7 jit_solution(10622195442796485779)
XLA Ops:
  0.0 0.0 copy-start
  0.0 2.2 %project.1 = (f32[2,64,256]{2,1,0:T(8,128)S(1)}, f32[2,64,256]{2,1,0:T(8,128)S(1)}) custom-call(bf16[2,3,1,512,256]{4,3,2,1,0:T(8,128)(2,1)} %vec_hbm.1, bf16[2,3,1,512,128]{4,3,2,1,0:T(8,128)(2,1)} %prop_hbm.1), custom_call_target="tpu_custom_call" | custom-call | tf_op jit(solution)/shard_map/project/pallas_call | solution.py:49
  2.2 0.0 copy-start.1
  2.2 0.0 copy-start.2
  2.2 3.1 %collective-permute-start = (f32[2,64,256]{2,1,0:T(8,128)S(1)}, f32[2,64,256]{2,1,0:T(8,128)S(1)}, u32[]{:S(2)}, u32[]{:S(2)}) collective-permute-start(f32[2,64,256]{2,1,0:T(8,128)S(1)} %get-tuple-element.10), channel_id=1, source_target_pairs={{0,1},{1,0},{2,3},{3,2},{4,5},{5,4},{6,7},{7,6},{8,9},{9,8},{10,11... | collective-permute-start | bytes 393224 | tf_op jit(solution)/shard_map/ppermute | solution.py:165
  5.3 3.5 %collective-permute-done = f32[2,64,256]{2,1,0:T(8,128)S(1)} collective-permute-done((f32[2,64,256]{2,1,0:T(8,128)S(1)}, f32[2,64,256]{2,1,0:T(8,128)S(1)}, u32[]{:S(2)}, u32[]{:S(2)}) %collective-permute-start) | collective-permute-done | bytes 131104 | tf_op jit(solution)/shard_map/ppermute | solution.py:165
  8.8 1.7 %collective-permute-start.1 = (bf16[1,2,64,256]{3,2,1,0:T(8,128)(2,1)S(1)}, bf16[1,2,64,256]{3,2,1,0:T(8,128)(2,1)S(1)}, u32[]{:S(2)}, u32[]{:S(2)}) collective-permute-start(bf16[1,2,64,256]{3,2,1,0:T(8,128)(2,1)S(1)} %get-tuple-element.13), channel_id=1, source_target_pairs={{0,8},{1,9},{2,10},{3,11},{4,20},{5,21},{6,22},{7,23},{8,0},{9,1},... | collective-permute-start | bytes 196616 | tf_op jit(solution)/shard_map/ppermute | solution.py:165
  10.5 2.6 %collective-permute-start.3 = (f32[2,64,256]{2,1,0:T(8,128)S(1)}, f32[2,64,256]{2,1,0:T(8,128)S(1)}, u32[]{:S(2)}, u32[]{:S(2)}) collective-permute-start(f32[2,64,256]{2,1,0:T(8,128)S(1)} %get-tuple-element.14.own_ref), channel_id=1, source_target_pairs={{0,2},{1,3},{2,0},{3,1},{4,6},{5,7},{6,4},{7,5},{8,10},{9,11},{10,... | collective-permute-start | bytes 393224 | tf_op jit(solution)/shard_map/ppermute | solution.py:165
  13.1 0.0 collective-permute-done.1
  13.2 0.1 collective-permute-start.2
  13.2 1.8 %collective-permute-start.4 = (bf16[2,2,64,256]{3,2,1,0:T(8,128)(2,1)S(1)}, bf16[2,2,64,256]{3,2,1,0:T(8,128)(2,1)S(1)}, u32[]{:S(2)}, u32[]{:S(2)}) collective-permute-start(bf16[2,2,64,256]{3,2,1,0:T(8,128)(2,1)S(1)} %pad_maximum_fusion.refs_0_), channel_id=1, source_target_pairs={{0,4},{1,5},{2,6},{3,7},{4,0},{5,1},{6,2},{7,3},{8,12},{9,13},{10,... | collective-permute-start | bytes 393224 | tf_op jit(solution)/shard_map/ppermute | solution.py:165
  15.0 3.4 %collective-permute-done.3.other_ref = f32[2,64,256]{2,1,0:T(8,128)S(1)} collective-permute-done((f32[2,64,256]{2,1,0:T(8,128)S(1)}, f32[2,64,256]{2,1,0:T(8,128)S(1)}, u32[]{:S(2)}, u32[]{:S(2)}) %collective-permute-start.3) | collective-permute-done | bytes 131104 | tf_op jit(solution)/shard_map/ppermute | solution.py:165
  18.3 0.0 collective-permute-done.2.refs_1_
  18.3 0.0 collective-permute-start.5
  18.4 0.0 copy-done
  18.4 0.8 %mix.1.mixed_ref = f32[8,2,64,256]{3,2,1,0:T(8,128)S(1)} custom-call(f32[2,64,256]{2,1,0:T(8,128)S(1)} %get-tuple-element.14.own_ref, f32[2,64,256]{2,1,0:T(8,128)S(1)} %collective-permute-done.3.other_ref, bf16[1,8,2,256,256]{4,3,2,1,0:T(8,128)(2,1)S(1)} %copy-done), custom_call_target="tpu_custom_call" | custom-call | flops 268435456 | bytes 262144 | tf_op jit(solution)/shard_map/mix/pallas_call | solution.py:88
  19.2 0.0 collective-permute-done.4.refs_2_
  19.2 0.5 %collective-permute-done.5.refs_3_ = bf16[2,2,64,256]{3,2,1,0:T(8,128)(2,1)S(1)} collective-permute-done((bf16[2,2,64,256]{3,2,1,0:T(8,128)(2,1)S(1)}, bf16[2,2,64,256]{3,2,1,0:T(8,128)(2,1)S(1)}, u32[]{:S(2)}, u32[]{:S(2)}) %collective-permute-start.5) | collective-permute-done | bytes 131104 | tf_op jit(solution)/shard_map/ppermute | solution.py:165
  19.7 0.0 copy-done.1
  19.7 0.0 copy-done.2
  19.7 1.0 %trace.1 = f32[2,16,128]{2,1,0:T(8,128)S(1)} custom-call(s32[1,16]{1,0:T(1,128)S(1)} %copy-done.1, s32[1,16]{1,0:T(1,128)S(1)} %copy-done.2, f32[8,2,64,256]{3,2,1,0:T(8,128)S(1)} %mix.1.mixed_ref, bf16[2,2,64,256]{3,2,1,0:T(8,128)(2,1)S(1)} %pad_maximum_fusion.refs_0_, bf16[2,2,64,256]{3,2,1,0:T(8,128)(2,1)S(1)} %collective-permute-done.2.refs_1_, ...), custom_call_target="tpu_custom_call" | custom-call | tf_op jit(solution)/shard_map/trace/pallas_call | solution.py:138
  20.7 0.8 %collective-permute-start.6 = (f32[2,16,128]{2,1,0:T(8,128)S(1)}, f32[2,16,128]{2,1,0:T(8,128)S(1)}, u32[]{:S(2)}, u32[]{:S(2)}) collective-permute-start(f32[2,16,128]{2,1,0:T(8,128)S(1)} %trace.1), channel_id=1, source_target_pairs={{0,5},{1,4},{2,7},{3,6},{4,1},{5,0},{6,3},{7,2},{8,13},{9,12},{10,... | collective-permute-start | bytes 49160 | tf_op jit(solution)/shard_map/ppermute | solution.py:165
  21.5 0.4 %collective-permute-start.7 = (f32[2,16,128]{2,1,0:T(8,128)S(1)}, f32[2,16,128]{2,1,0:T(8,128)S(1)}, u32[]{:S(2)}, u32[]{:S(2)}) collective-permute-start(f32[2,16,128]{2,1,0:T(8,128)S(1)} %trace.1), channel_id=1, source_target_pairs={{0,4},{1,5},{2,6},{3,7},{4,0},{5,1},{6,2},{7,3},{8,12},{9,13},{10,... | collective-permute-start | bytes 49160 | tf_op jit(solution)/shard_map/ppermute | solution.py:165
  21.9 2.1 %collective-permute-done.6 = f32[2,16,128]{2,1,0:T(8,128)S(1)} collective-permute-done((f32[2,16,128]{2,1,0:T(8,128)S(1)}, f32[2,16,128]{2,1,0:T(8,128)S(1)}, u32[]{:S(2)}, u32[]{:S(2)}) %collective-permute-start.6) | collective-permute-done | bytes 16416 | tf_op jit(solution)/shard_map/ppermute | solution.py:165
  23.9 0.0 collective-permute-done.7
  23.9 2.1 %collective-permute-start.8 = (f32[2,16,128]{2,1,0:T(8,128)S(1)}, f32[2,16,128]{2,1,0:T(8,128)S(1)}, u32[]{:S(2)}, u32[]{:S(2)}) collective-permute-start(f32[2,16,128]{2,1,0:T(8,128)S(1)} %add.10), channel_id=1, source_target_pairs={{0,6},{1,7},{2,4},{3,5},{4,2},{5,3},{6,0},{7,1},{8,14},{9,15},{10,... | collective-permute-start | bytes 49160 | tf_op jit(solution)/shard_map/ppermute | solution.py:165
  26.0 0.2 collective-permute-start.9
  26.2 1.9 %collective-permute-done.8 = f32[2,16,128]{2,1,0:T(8,128)S(1)} collective-permute-done((f32[2,16,128]{2,1,0:T(8,128)S(1)}, f32[2,16,128]{2,1,0:T(8,128)S(1)}, u32[]{:S(2)}, u32[]{:S(2)}) %collective-permute-start.8) | collective-permute-done | bytes 16416 | tf_op jit(solution)/shard_map/ppermute | solution.py:165
  28.1 0.0 collective-permute-done.9
  28.1 0.6 %add_reduce_fusion = f32[2,16]{1,0:T(2,128)} fusion(f32[2,16,128]{2,1,0:T(8,128)S(1)} %collective-permute-done.8, f32[2,16,128]{2,1,0:T(8,128)S(1)} %collective-permute-done.9), kind=kLoop, calls=%fused_computation.2 | loop fusion | flops 8160 | bytes 32896 | tf_op jit(solution)/shard_map/reduce_sum | solution.py:191
  (3 shorter events, 0.0 us)
Async XLA Ops:
  0.0 18.4 %copy-start = (bf16[1,8,2,256,256]{4,3,2,1,0:T(8,128)(2,1)S(1)}, bf16[1,8,2,256,256]{4,3,2,1,0:T(8,128)(2,1)}, u32[]{:S(2)}) copy-start(bf16[1,8,2,256,256]{4,3,2,1,0:T(8,128)(2,1)} %elem_ref.1) | copy-start | bytes 6291460
  2.2 17.5 %copy-start.1 = (s32[1,16]{1,0:T(1,128)S(1)}, s32[1,16]{1,0:T(1,128)}, u32[]{:S(2)}) copy-start(s32[1,16]{1,0:T(1,128)} %sink_ref.1) | copy-start | bytes 196
  2.2 17.5 %copy-start.2 = (s32[1,16]{1,0:T(1,128)S(1)}, s32[1,16]{1,0:T(1,128)}, u32[]{:S(2)}) copy-start(s32[1,16]{1,0:T(1,128)} %mom_ref.1) | copy-start | bytes 196
  2.2 6.6 %collective-permute-start = (f32[2,64,256]{2,1,0:T(8,128)S(1)}, f32[2,64,256]{2,1,0:T(8,128)S(1)}, u32[]{:S(2)}, u32[]{:S(2)}) collective-permute-start(f32[2,64,256]{2,1,0:T(8,128)S(1)} %get-tuple-element.10), channel_id=1, source_target_pairs={{0,1},{1,0},{2,3},{3,2},{4,5},{5,4},{6,7},{7,6},{8,9},{9,8},{10,11... | collective-permute-start | bytes 393224 | tf_op jit(solution)/shard_map/ppermute | solution.py:165
  8.8 4.3 %collective-permute-start.1 = (bf16[1,2,64,256]{3,2,1,0:T(8,128)(2,1)S(1)}, bf16[1,2,64,256]{3,2,1,0:T(8,128)(2,1)S(1)}, u32[]{:S(2)}, u32[]{:S(2)}) collective-permute-start(bf16[1,2,64,256]{3,2,1,0:T(8,128)(2,1)S(1)} %get-tuple-element.13), channel_id=1, source_target_pairs={{0,8},{1,9},{2,10},{3,11},{4,20},{5,21},{6,22},{7,23},{8,0},{9,1},... | collective-permute-start | bytes 196616 | tf_op jit(solution)/shard_map/ppermute | solution.py:165
  10.5 7.8 %collective-permute-start.3 = (f32[2,64,256]{2,1,0:T(8,128)S(1)}, f32[2,64,256]{2,1,0:T(8,128)S(1)}, u32[]{:S(2)}, u32[]{:S(2)}) collective-permute-start(f32[2,64,256]{2,1,0:T(8,128)S(1)} %get-tuple-element.14.own_ref), channel_id=1, source_target_pairs={{0,2},{1,3},{2,0},{3,1},{4,6},{5,7},{6,4},{7,5},{8,10},{9,11},{10,... | collective-permute-start | bytes 393224 | tf_op jit(solution)/shard_map/ppermute | solution.py:165
  13.2 5.2 %collective-permute-start.2 = (bf16[2,2,64,256]{3,2,1,0:T(8,128)(2,1)S(1)}, bf16[2,2,64,256]{3,2,1,0:T(8,128)(2,1)S(1)}, u32[]{:S(2)}, u32[]{:S(2)}) collective-permute-start(bf16[2,2,64,256]{3,2,1,0:T(8,128)(2,1)S(1)} %pad_maximum_fusion.refs_0_), channel_id=1, source_target_pairs={{0,20},{1,21},{2,22},{3,23},{4,8},{5,9},{6,10},{7,11},{8,28},{9,29... | collective-permute-start | bytes 393224 | tf_op jit(solution)/shard_map/ppermute | solution.py:165
  13.2 6.0 %collective-permute-start.4 = (bf16[2,2,64,256]{3,2,1,0:T(8,128)(2,1)S(1)}, bf16[2,2,64,256]{3,2,1,0:T(8,128)(2,1)S(1)}, u32[]{:S(2)}, u32[]{:S(2)}) collective-permute-start(bf16[2,2,64,256]{3,2,1,0:T(8,128)(2,1)S(1)} %pad_maximum_fusion.refs_0_), channel_id=1, source_target_pairs={{0,4},{1,5},{2,6},{3,7},{4,0},{5,1},{6,2},{7,3},{8,12},{9,13},{10,... | collective-permute-start | bytes 393224 | tf_op jit(solution)/shard_map/ppermute | solution.py:165
  18.3 1.3 %collective-permute-start.5 = (bf16[2,2,64,256]{3,2,1,0:T(8,128)(2,1)S(1)}, bf16[2,2,64,256]{3,2,1,0:T(8,128)(2,1)S(1)}, u32[]{:S(2)}, u32[]{:S(2)}) collective-permute-start(bf16[2,2,64,256]{3,2,1,0:T(8,128)(2,1)S(1)} %collective-permute-done.2.refs_1_), channel_id=1, source_target_pairs={{0,4},{1,5},{2,6},{3,7},{4,0},{5,1},{6,2},{7,3},{8,12},{9,13},{10,... | collective-permute-start | bytes 393224 | tf_op jit(solution)/shard_map/ppermute | solution.py:165
  20.7 3.2 %collective-permute-start.6 = (f32[2,16,128]{2,1,0:T(8,128)S(1)}, f32[2,16,128]{2,1,0:T(8,128)S(1)}, u32[]{:S(2)}, u32[]{:S(2)}) collective-permute-start(f32[2,16,128]{2,1,0:T(8,128)S(1)} %trace.1), channel_id=1, source_target_pairs={{0,5},{1,4},{2,7},{3,6},{4,1},{5,0},{6,3},{7,2},{8,13},{9,12},{10,... | collective-permute-start | bytes 49160 | tf_op jit(solution)/shard_map/ppermute | solution.py:165
  21.5 2.4 %collective-permute-start.7 = (f32[2,16,128]{2,1,0:T(8,128)S(1)}, f32[2,16,128]{2,1,0:T(8,128)S(1)}, u32[]{:S(2)}, u32[]{:S(2)}) collective-permute-start(f32[2,16,128]{2,1,0:T(8,128)S(1)} %trace.1), channel_id=1, source_target_pairs={{0,4},{1,5},{2,6},{3,7},{4,0},{5,1},{6,2},{7,3},{8,12},{9,13},{10,... | collective-permute-start | bytes 49160 | tf_op jit(solution)/shard_map/ppermute | solution.py:165
  23.9 4.1 %collective-permute-start.8 = (f32[2,16,128]{2,1,0:T(8,128)S(1)}, f32[2,16,128]{2,1,0:T(8,128)S(1)}, u32[]{:S(2)}, u32[]{:S(2)}) collective-permute-start(f32[2,16,128]{2,1,0:T(8,128)S(1)} %add.10), channel_id=1, source_target_pairs={{0,6},{1,7},{2,4},{3,5},{4,2},{5,3},{6,0},{7,1},{8,14},{9,15},{10,... | collective-permute-start | bytes 49160 | tf_op jit(solution)/shard_map/ppermute | solution.py:165
  26.0 2.0 %collective-permute-start.9 = (f32[2,16,128]{2,1,0:T(8,128)S(1)}, f32[2,16,128]{2,1,0:T(8,128)S(1)}, u32[]{:S(2)}, u32[]{:S(2)}) collective-permute-start(f32[2,16,128]{2,1,0:T(8,128)S(1)} %add.10), channel_id=1, source_target_pairs={{0,4},{1,5},{2,6},{3,7},{4,0},{5,1},{6,2},{7,3},{8,12},{9,13},{10,... | collective-permute-start | bytes 49160 | tf_op jit(solution)/shard_map/ppermute | solution.py:165

commit v4 on v3

--- a/solution.py
+++ b/solution.py
@@ -129,7 +129,7 @@
             rows, lanes = value.shape
             value = jnp.sum(value.reshape(rows // 8, 8, lanes), axis=0)
             sums_ref[o, k] = sum(value[:, i * 128 : (i + 1) * 128] for i in range(lanes // 128))
-    out_ref[...] = jnp.sum(sums_ref[...], axis=2)
+    out_ref[...] = jnp.sum(jnp.sum(sums_ref[...], axis=2), axis=-1)
 
 
 def trace(orders, sink_times, momenta, mixed, groups):
@@ -137,9 +137,8 @@
     per_group = groups[0].shape[0]
     return pl.pallas_call(
         functools.partial(trace_kernel, orders),
-        out_shape=jax.ShapeDtypeStruct((2, items, 128), jnp.float32),
-        in_specs=[pl.BlockSpec(memory_space=pltpu.SMEM)] * 2
-        + [pl.BlockSpec(memory_space=pltpu.VMEM)] * (1 + len(groups)),
+        out_shape=jax.ShapeDtypeStruct((2, items), jnp.float32),
+        in_specs=[pl.BlockSpec(memory_space=pltpu.VMEM)] * (3 + len(groups)),
         out_specs=pl.BlockSpec(memory_space=pltpu.VMEM),
         scratch_shapes=[
             pltpu.VMEM((len(groups) * per_group,) + groups[0].shape[1:], jnp.bfloat16),
@@ -188,7 +187,7 @@
     for bit in range(space_bits):
         far = exchange(partial, lambda t, s: (t ^ 1, s ^ (1 << bit)))
         partial = far + exchange(partial, cross)
-    return jnp.sum(partial, axis=-1)[:, None, :]
+    return partial[:, None, :]
 
 
 def by_collectives(eigvecs, propagator, elementals, sink_times, momenta):

time: 28.9 us -> 27.9 us (0.965)
  Pallas kernels: 3.96 us -> 3.58 us
  waiting for transfers between devices: 11.3 us -> 11 us
    reduce_sum x1 -> x0, other arithmetic: 0.65 us -> none  [by_exchanges(): return jnp.sum(partial, axis=-1)[:, None, :]]
    add x1 -> x2, other arithmetic: 0.01 us -> 0.57 us  [by_exchanges(): partial = far + exchange(partial, cross)]
    ppermute x10, waiting for transfers between devices: 11.3 us -> 11 us  [exchange(): return lax.ppermute(value, axes, pairs)]
    pallas_call x1, Pallas kernels: 0.98 us -> 0.61 us  [trace(): pl.pallas_call(functools.partial(trace_kernel, orders), out_shape=jax.Sha...]
where the time goes in v4:
time: 27.9 us; the launch traced here: 27.8 us
  starting transfers between devices  12.5 us (45%)
  waiting for transfers between devices  11 us (39%)
  Pallas kernels  3.58 us (13%)
  other arithmetic  0.6 us (2%)
    ppermute x10, starting transfers between devices, exchange(): return lax.ppermute(value, axes, pairs)  12.5 us
    ppermute x10, waiting for transfers between devices, exchange(): return lax.ppermute(value, axes, pairs)  11 us
    pallas_call x1, Pallas kernels, project(): pl.pallas_call(project_kernel, out_shape=(out, out), in_specs=[pl.BlockSp...  2.16 us
    pallas_call x1, Pallas kernels, mix(): pl.pallas_call(mix_kernel, out_shape=jax.ShapeDtypeStruct((momenta,) + ow...  0.82 us
    pallas_call x1, Pallas kernels, trace(): pl.pallas_call(functools.partial(trace_kernel, orders), out_shape=jax.Sha...  0.61 us
    add x2, other arithmetic, by_exchanges(): partial = far + exchange(partial, cross)  0.57 us
  transfers between devices with their start and end apart: 10, of which 5 were waited for; matrix products, arithmetic and copies ran while one was open for 0% of the time, Pallas kernels for 3%

profile of v4, /device:TPU:0, one launch (start us, length us, event | category | flops | bytes accessed | tf_op | source)
XLA Modules:
  0.0 27.8 jit_solution(9767002256809445804)
XLA Ops:
  0.0 0.0 copy-start
  0.0 2.2 %project.1 = (f32[2,64,256]{2,1,0:T(8,128)S(1)}, f32[2,64,256]{2,1,0:T(8,128)S(1)}) custom-call(bf16[2,3,1,512,256]{4,3,2,1,0:T(8,128)(2,1)} %vec_hbm.1, bf16[2,3,1,512,128]{4,3,2,1,0:T(8,128)(2,1)} %prop_hbm.1), custom_call_target="tpu_custom_call" | custom-call | tf_op jit(solution)/shard_map/project/pallas_call | solution.py:49
  2.2 0.0 copy-start.1
  2.2 0.0 copy-start.2
  2.2 3.1 %collective-permute-start = (f32[2,64,256]{2,1,0:T(8,128)S(1)}, f32[2,64,256]{2,1,0:T(8,128)S(1)}, u32[]{:S(2)}, u32[]{:S(2)}) collective-permute-start(f32[2,64,256]{2,1,0:T(8,128)S(1)} %get-tuple-element.10), channel_id=1, source_target_pairs={{0,1},{1,0},{2,3},{3,2},{4,5},{5,4},{6,7},{7,6},{8,9},{9,8},{10,11... | collective-permute-start | bytes 393224 | tf_op jit(solution)/shard_map/ppermute | solution.py:164
  5.3 3.5 %collective-permute-done = f32[2,64,256]{2,1,0:T(8,128)S(1)} collective-permute-done((f32[2,64,256]{2,1,0:T(8,128)S(1)}, f32[2,64,256]{2,1,0:T(8,128)S(1)}, u32[]{:S(2)}, u32[]{:S(2)}) %collective-permute-start) | collective-permute-done | bytes 131104 | tf_op jit(solution)/shard_map/ppermute | solution.py:164
  8.8 1.7 %collective-permute-start.1 = (bf16[1,2,64,256]{3,2,1,0:T(8,128)(2,1)S(1)}, bf16[1,2,64,256]{3,2,1,0:T(8,128)(2,1)S(1)}, u32[]{:S(2)}, u32[]{:S(2)}) collective-permute-start(bf16[1,2,64,256]{3,2,1,0:T(8,128)(2,1)S(1)} %get-tuple-element.13), channel_id=1, source_target_pairs={{0,8},{1,9},{2,10},{3,11},{4,20},{5,21},{6,22},{7,23},{8,0},{9,1},... | collective-permute-start | bytes 196616 | tf_op jit(solution)/shard_map/ppermute | solution.py:164
  10.5 2.6 %collective-permute-start.3 = (f32[2,64,256]{2,1,0:T(8,128)S(1)}, f32[2,64,256]{2,1,0:T(8,128)S(1)}, u32[]{:S(2)}, u32[]{:S(2)}) collective-permute-start(f32[2,64,256]{2,1,0:T(8,128)S(1)} %get-tuple-element.14.own_ref), channel_id=1, source_target_pairs={{0,2},{1,3},{2,0},{3,1},{4,6},{5,7},{6,4},{7,5},{8,10},{9,11},{10,... | collective-permute-start | bytes 393224 | tf_op jit(solution)/shard_map/ppermute | solution.py:164
  13.1 0.0 collective-permute-done.1
  13.2 0.1 collective-permute-start.2
  13.2 1.8 %collective-permute-start.4 = (bf16[2,2,64,256]{3,2,1,0:T(8,128)(2,1)S(1)}, bf16[2,2,64,256]{3,2,1,0:T(8,128)(2,1)S(1)}, u32[]{:S(2)}, u32[]{:S(2)}) collective-permute-start(bf16[2,2,64,256]{3,2,1,0:T(8,128)(2,1)S(1)} %pad_maximum_fusion.refs_0_), channel_id=1, source_target_pairs={{0,4},{1,5},{2,6},{3,7},{4,0},{5,1},{6,2},{7,3},{8,12},{9,13},{10,... | collective-permute-start | bytes 393224 | tf_op jit(solution)/shard_map/ppermute | solution.py:164
  15.0 3.4 %collective-permute-done.3.other_ref = f32[2,64,256]{2,1,0:T(8,128)S(1)} collective-permute-done((f32[2,64,256]{2,1,0:T(8,128)S(1)}, f32[2,64,256]{2,1,0:T(8,128)S(1)}, u32[]{:S(2)}, u32[]{:S(2)}) %collective-permute-start.3) | collective-permute-done | bytes 131104 | tf_op jit(solution)/shard_map/ppermute | solution.py:164
  18.3 0.0 collective-permute-done.2.refs_1_
  18.3 0.0 collective-permute-start.5
  18.4 0.0 copy-done
  18.4 0.8 %mix.1.mixed_ref = f32[8,2,64,256]{3,2,1,0:T(8,128)S(1)} custom-call(f32[2,64,256]{2,1,0:T(8,128)S(1)} %get-tuple-element.14.own_ref, f32[2,64,256]{2,1,0:T(8,128)S(1)} %collective-permute-done.3.other_ref, bf16[1,8,2,256,256]{4,3,2,1,0:T(8,128)(2,1)S(1)} %copy-done), custom_call_target="tpu_custom_call" | custom-call | flops 268435456 | bytes 262144 | tf_op jit(solution)/shard_map/mix/pallas_call | solution.py:88
  19.2 0.0 collective-permute-done.4.refs_2_
  19.2 0.5 %collective-permute-done.5.refs_3_ = bf16[2,2,64,256]{3,2,1,0:T(8,128)(2,1)S(1)} collective-permute-done((bf16[2,2,64,256]{3,2,1,0:T(8,128)(2,1)S(1)}, bf16[2,2,64,256]{3,2,1,0:T(8,128)(2,1)S(1)}, u32[]{:S(2)}, u32[]{:S(2)}) %collective-permute-start.5) | collective-permute-done | bytes 131104 | tf_op jit(solution)/shard_map/ppermute | solution.py:164
  19.7 0.0 copy-done.1
  19.7 0.0 copy-done.2
  19.7 0.6 %trace.1 = f32[2,16]{1,0:T(2,128)S(1)} custom-call(s32[1,16]{1,0:T(1,128)S(1)} %copy-done.1, s32[1,16]{1,0:T(1,128)S(1)} %copy-done.2, f32[8,2,64,256]{3,2,1,0:T(8,128)S(1)} %mix.1.mixed_ref, bf16[2,2,64,256]{3,2,1,0:T(8,128)(2,1)S(1)} %pad_maximum_fusion.refs_0_, bf16[2,2,64,256]{3,2,1,0:T(8,128)(2,1)S(1)} %collective-permute-done.2.refs_1_, ...), custom_call_target="tpu_custom_call" | custom-call | tf_op jit(solution)/shard_map/trace/pallas_call | solution.py:138
  20.3 0.7 %collective-permute-start.6 = (f32[2,16]{1,0:T(2,128)S(1)}, f32[2,16]{1,0:T(2,128)S(1)}, u32[]{:S(2)}, u32[]{:S(2)}) collective-permute-start(f32[2,16]{1,0:T(2,128)S(1)} %trace.1), channel_id=1, source_target_pairs={{0,5},{1,4},{2,7},{3,6},{4,1},{5,0},{6,3},{7,2},{8,13},{9,12},{10,... | collective-permute-start | bytes 392 | tf_op jit(solution)/shard_map/ppermute | solution.py:164
  21.1 0.4 %collective-permute-start.7 = (f32[2,16]{1,0:T(2,128)S(1)}, f32[2,16]{1,0:T(2,128)S(1)}, u32[]{:S(2)}, u32[]{:S(2)}) collective-permute-start(f32[2,16]{1,0:T(2,128)S(1)} %trace.1), channel_id=1, source_target_pairs={{0,4},{1,5},{2,6},{3,7},{4,0},{5,1},{6,2},{7,3},{8,12},{9,13},{10,... | collective-permute-start | bytes 392 | tf_op jit(solution)/shard_map/ppermute | solution.py:164
  21.4 1.9 %collective-permute-done.6 = f32[2,16]{1,0:T(2,128)S(1)} collective-permute-done((f32[2,16]{1,0:T(2,128)S(1)}, f32[2,16]{1,0:T(2,128)S(1)}, u32[]{:S(2)}, u32[]{:S(2)}) %collective-permute-start.6) | collective-permute-done | bytes 160 | tf_op jit(solution)/shard_map/ppermute | solution.py:164
  23.3 0.0 collective-permute-done.7
  23.3 2.0 %collective-permute-start.8 = (f32[2,16]{1,0:T(2,128)S(1)}, f32[2,16]{1,0:T(2,128)S(1)}, u32[]{:S(2)}, u32[]{:S(2)}) collective-permute-start(f32[2,16]{1,0:T(2,128)S(1)} %add.10), channel_id=1, source_target_pairs={{0,6},{1,7},{2,4},{3,5},{4,2},{5,3},{6,0},{7,1},{8,14},{9,15},{10,... | collective-permute-start | bytes 392 | tf_op jit(solution)/shard_map/ppermute | solution.py:164
  25.3 0.2 collective-permute-start.9
  25.5 1.7 %collective-permute-done.8 = f32[2,16]{1,0:T(2,128)S(1)} collective-permute-done((f32[2,16]{1,0:T(2,128)S(1)}, f32[2,16]{1,0:T(2,128)S(1)}, u32[]{:S(2)}, u32[]{:S(2)}) %collective-permute-start.8) | collective-permute-done | bytes 160 | tf_op jit(solution)/shard_map/ppermute | solution.py:164
  27.2 0.0 collective-permute-done.9
  27.2 0.6 %add.11 = f32[2,16]{1,0:T(2,128)} add(f32[2,16]{1,0:T(2,128)S(1)} %collective-permute-done.8, f32[2,16]{1,0:T(2,128)S(1)} %collective-permute-done.9) | non-fusion elementwise | flops 32 | bytes 384 | tf_op jit(solution)/shard_map/add | solution.py:189
  (3 shorter events, 0.0 us)
Async XLA Ops:
  0.0 18.4 %copy-start = (bf16[1,8,2,256,256]{4,3,2,1,0:T(8,128)(2,1)S(1)}, bf16[1,8,2,256,256]{4,3,2,1,0:T(8,128)(2,1)}, u32[]{:S(2)}) copy-start(bf16[1,8,2,256,256]{4,3,2,1,0:T(8,128)(2,1)} %elem_ref.1) | copy-start | bytes 6291460
  2.2 17.5 %copy-start.1 = (s32[1,16]{1,0:T(1,128)S(1)}, s32[1,16]{1,0:T(1,128)}, u32[]{:S(2)}) copy-start(s32[1,16]{1,0:T(1,128)} %sink_ref.1) | copy-start | bytes 196
  2.2 17.5 %copy-start.2 = (s32[1,16]{1,0:T(1,128)S(1)}, s32[1,16]{1,0:T(1,128)}, u32[]{:S(2)}) copy-start(s32[1,16]{1,0:T(1,128)} %mom_ref.1) | copy-start | bytes 196
  2.2 6.6 %collective-permute-start = (f32[2,64,256]{2,1,0:T(8,128)S(1)}, f32[2,64,256]{2,1,0:T(8,128)S(1)}, u32[]{:S(2)}, u32[]{:S(2)}) collective-permute-start(f32[2,64,256]{2,1,0:T(8,128)S(1)} %get-tuple-element.10), channel_id=1, source_target_pairs={{0,1},{1,0},{2,3},{3,2},{4,5},{5,4},{6,7},{7,6},{8,9},{9,8},{10,11... | collective-permute-start | bytes 393224 | tf_op jit(solution)/shard_map/ppermute | solution.py:164
  8.8 4.3 %collective-permute-start.1 = (bf16[1,2,64,256]{3,2,1,0:T(8,128)(2,1)S(1)}, bf16[1,2,64,256]{3,2,1,0:T(8,128)(2,1)S(1)}, u32[]{:S(2)}, u32[]{:S(2)}) collective-permute-start(bf16[1,2,64,256]{3,2,1,0:T(8,128)(2,1)S(1)} %get-tuple-element.13), channel_id=1, source_target_pairs={{0,8},{1,9},{2,10},{3,11},{4,20},{5,21},{6,22},{7,23},{8,0},{9,1},... | collective-permute-start | bytes 196616 | tf_op jit(solution)/shard_map/ppermute | solution.py:164
  10.5 7.8 %collective-permute-start.3 = (f32[2,64,256]{2,1,0:T(8,128)S(1)}, f32[2,64,256]{2,1,0:T(8,128)S(1)}, u32[]{:S(2)}, u32[]{:S(2)}) collective-permute-start(f32[2,64,256]{2,1,0:T(8,128)S(1)} %get-tuple-element.14.own_ref), channel_id=1, source_target_pairs={{0,2},{1,3},{2,0},{3,1},{4,6},{5,7},{6,4},{7,5},{8,10},{9,11},{10,... | collective-permute-start | bytes 393224 | tf_op jit(solution)/shard_map/ppermute | solution.py:164
  13.2 5.2 %collective-permute-start.2 = (bf16[2,2,64,256]{3,2,1,0:T(8,128)(2,1)S(1)}, bf16[2,2,64,256]{3,2,1,0:T(8,128)(2,1)S(1)}, u32[]{:S(2)}, u32[]{:S(2)}) collective-permute-start(bf16[2,2,64,256]{3,2,1,0:T(8,128)(2,1)S(1)} %pad_maximum_fusion.refs_0_), channel_id=1, source_target_pairs={{0,20},{1,21},{2,22},{3,23},{4,8},{5,9},{6,10},{7,11},{8,28},{9,29... | collective-permute-start | bytes 393224 | tf_op jit(solution)/shard_map/ppermute | solution.py:164
  13.2 6.0 %collective-permute-start.4 = (bf16[2,2,64,256]{3,2,1,0:T(8,128)(2,1)S(1)}, bf16[2,2,64,256]{3,2,1,0:T(8,128)(2,1)S(1)}, u32[]{:S(2)}, u32[]{:S(2)}) collective-permute-start(bf16[2,2,64,256]{3,2,1,0:T(8,128)(2,1)S(1)} %pad_maximum_fusion.refs_0_), channel_id=1, source_target_pairs={{0,4},{1,5},{2,6},{3,7},{4,0},{5,1},{6,2},{7,3},{8,12},{9,13},{10,... | collective-permute-start | bytes 393224 | tf_op jit(solution)/shard_map/ppermute | solution.py:164
  18.3 1.3 %collective-permute-start.5 = (bf16[2,2,64,256]{3,2,1,0:T(8,128)(2,1)S(1)}, bf16[2,2,64,256]{3,2,1,0:T(8,128)(2,1)S(1)}, u32[]{:S(2)}, u32[]{:S(2)}) collective-permute-start(bf16[2,2,64,256]{3,2,1,0:T(8,128)(2,1)S(1)} %collective-permute-done.2.refs_1_), channel_id=1, source_target_pairs={{0,4},{1,5},{2,6},{3,7},{4,0},{5,1},{6,2},{7,3},{8,12},{9,13},{10,... | collective-permute-start | bytes 393224 | tf_op jit(solution)/shard_map/ppermute | solution.py:164
  20.3 3.0 %collective-permute-start.6 = (f32[2,16]{1,0:T(2,128)S(1)}, f32[2,16]{1,0:T(2,128)S(1)}, u32[]{:S(2)}, u32[]{:S(2)}) collective-permute-start(f32[2,16]{1,0:T(2,128)S(1)} %trace.1), channel_id=1, source_target_pairs={{0,5},{1,4},{2,7},{3,6},{4,1},{5,0},{6,3},{7,2},{8,13},{9,12},{10,... | collective-permute-start | bytes 392 | tf_op jit(solution)/shard_map/ppermute | solution.py:164
  21.1 2.3 %collective-permute-start.7 = (f32[2,16]{1,0:T(2,128)S(1)}, f32[2,16]{1,0:T(2,128)S(1)}, u32[]{:S(2)}, u32[]{:S(2)}) collective-permute-start(f32[2,16]{1,0:T(2,128)S(1)} %trace.1), channel_id=1, source_target_pairs={{0,4},{1,5},{2,6},{3,7},{4,0},{5,1},{6,2},{7,3},{8,12},{9,13},{10,... | collective-permute-start | bytes 392 | tf_op jit(solution)/shard_map/ppermute | solution.py:164
  23.3 3.9 %collective-permute-start.8 = (f32[2,16]{1,0:T(2,128)S(1)}, f32[2,16]{1,0:T(2,128)S(1)}, u32[]{:S(2)}, u32[]{:S(2)}) collective-permute-start(f32[2,16]{1,0:T(2,128)S(1)} %add.10), channel_id=1, source_target_pairs={{0,6},{1,7},{2,4},{3,5},{4,2},{5,3},{6,0},{7,1},{8,14},{9,15},{10,... | collective-permute-start | bytes 392 | tf_op jit(solution)/shard_map/ppermute | solution.py:164
  25.3 1.9 %collective-permute-start.9 = (f32[2,16]{1,0:T(2,128)S(1)}, f32[2,16]{1,0:T(2,128)S(1)}, u32[]{:S(2)}, u32[]{:S(2)}) collective-permute-start(f32[2,16]{1,0:T(2,128)S(1)} %add.10), channel_id=1, source_target_pairs={{0,4},{1,5},{2,6},{3,7},{4,0},{5,1},{6,2},{7,3},{8,12},{9,13},{10,... | collective-permute-start | bytes 392 | tf_op jit(solution)/shard_map/ppermute | solution.py:164

commit v5 on v4

--- a/solution.py
+++ b/solution.py
@@ -38,17 +38,22 @@
     for out_ref, which in ((send_ref, 1 - mine), (keep_ref, mine)):
         top = pl.ds(pl.multiple_of(which * half, half), half)
         low = pl.ds(pl.multiple_of(columns + which * half, half), half)
-        out_ref[0] = acc_ref[top, :vec_count] + acc_ref[low, vec_count:]
-        out_ref[1] = acc_ref[low, :vec_count] - acc_ref[top, vec_count:]
+        real = acc_ref[top, :vec_count] + acc_ref[low, vec_count:]
+        imag = acc_ref[low, :vec_count] - acc_ref[top, vec_count:]
+        out_ref[0] = real.astype(out_ref.dtype)
+        out_ref[1] = imag.astype(out_ref.dtype)
 
 
 def project(eigvecs, propagator):
     _, colours, _, sites, vec_count = eigvecs.shape
     columns = propagator.shape[-1]
-    out = jax.ShapeDtypeStruct((2, columns // 2, vec_count), jnp.float32)
+    shape = (2, columns // 2, vec_count)
     return pl.pallas_call(
         project_kernel,
-        out_shape=(out, out),
+        out_shape=(
+            jax.ShapeDtypeStruct(shape, jnp.float32),
+            jax.ShapeDtypeStruct(shape, jnp.bfloat16),
+        ),
         in_specs=[pl.BlockSpec(memory_space=pl.ANY)] * 2,
         out_specs=[pl.BlockSpec(memory_space=pltpu.VMEM)] * 2,
         scratch_shapes=[
@@ -57,13 +62,9 @@
             pltpu.VMEM((2 * columns, 2 * vec_count), jnp.float32),
             pltpu.SemaphoreType.DMA((2, colours)),
         ],
-        compiler_params=pltpu.CompilerParams(vmem_limit_bytes=53 * MIB),
+        compiler_params=pltpu.CompilerParams(vmem_limit_bytes=107 * MIB // 2),
         name="project",
     )(eigvecs, propagator)
-
-
-def rounded(value):
-    return value.astype(jnp.bfloat16).astype(jnp.float32)
 
 
 def mix_kernel(own_ref, other_ref, elem_ref, mixed_ref):
@@ -78,8 +79,8 @@
             )
             for r in range(2)
         )
-        mixed_ref[p, 0] = rounded(by_real[:half] - by_imag[half:])
-        mixed_ref[p, 1] = rounded(by_imag[:half] + by_real[half:])
+        mixed_ref[p, 0] = by_real[:half] - by_imag[half:]
+        mixed_ref[p, 1] = by_imag[:half] + by_real[half:]
 
 
 def mix(own, other, elementals):
@@ -167,7 +168,7 @@
         return exchange(value, lambda t, s: (t, s ^ (1 << bit)))
 
     keep, send = project(eigvecs, propagator)
-    own = keep + across(send, 0)
+    own = keep + across(send, 0).astype(jnp.float32)
     blocks = own.astype(jnp.bfloat16)[None]
     total, other = own, jnp.zeros_like(own)
     for bit in range(1, space_bits):

time: 27.9 us -> 26.7 us (0.957)
  waiting for transfers between devices: 11 us -> 8.97 us
  starting transfers between devices: 12.5 us -> 13.3 us
    ppermute x10, waiting for transfers between devices: 11 us -> 8.97 us  [exchange(): return lax.ppermute(value, axes, pairs)]
    ppermute x10, starting transfers between devices: 12.5 us -> 13.3 us  [exchange(): return lax.ppermute(value, axes, pairs)]
where the time goes in v5:
time: 26.7 us; the launch traced here: 26.5 us
  starting transfers between devices  13.3 us (50%)
  waiting for transfers between devices  8.97 us (34%)
  Pallas kernels  3.58 us (13%)
  other arithmetic  0.6 us (2%)
    ppermute x10, starting transfers between devices, exchange(): return lax.ppermute(value, axes, pairs)  13.3 us
    ppermute x10, waiting for transfers between devices, exchange(): return lax.ppermute(value, axes, pairs)  8.97 us
    pallas_call x1, Pallas kernels, project(): pl.pallas_call(project_kernel, out_shape=(jax.ShapeDtypeStruct(shape, jnp...  2.16 us
    pallas_call x1, Pallas kernels, mix(): pl.pallas_call(mix_kernel, out_shape=jax.ShapeDtypeStruct((momenta,) + ow...  0.81 us
    pallas_call x1, Pallas kernels, trace(): pl.pallas_call(functools.partial(trace_kernel, orders), out_shape=jax.Sha...  0.61 us
    add x2, other arithmetic, by_exchanges(): partial = far + exchange(partial, cross)  0.57 us
  transfers between devices with their start and end apart: 10, of which 5 were waited for; matrix products, arithmetic and copies ran while one was open for 0% of the time, Pallas kernels for 3%

profile of v5, /device:TPU:0, one launch (start us, length us, event | category | flops | bytes accessed | tf_op | source)
XLA Modules:
  0.0 26.5 jit_solution(4356645150575203486)
XLA Ops:
  0.0 0.0 copy-start
  0.0 2.2 %project.1 = (f32[2,64,256]{2,1,0:T(8,128)S(1)}, bf16[2,64,256]{2,1,0:T(8,128)(2,1)S(1)}) custom-call(bf16[2,3,1,512,256]{4,3,2,1,0:T(8,128)(2,1)} %vec_hbm.1, bf16[2,3,1,512,128]{4,3,2,1,0:T(8,128)(2,1)} %prop_hbm.1), custom_call_target="tpu_custom_call" | custom-call | tf_op jit(solution)/shard_map/project/pallas_call | solution.py:51
  2.2 0.0 copy-start.1
  2.2 0.0 copy-start.2
  2.2 3.1 %collective-permute-start = (bf16[2,64,256]{2,1,0:T(8,128)(2,1)S(1)}, bf16[2,64,256]{2,1,0:T(8,128)(2,1)S(1)}, u32[]{:S(2)}, u32[]{:S(2)}) collective-permute-start(bf16[2,64,256]{2,1,0:T(8,128)(2,1)S(1)} %get-tuple-element.10), channel_id=1, source_target_pairs={{0,1},{1,0},{2,3},{3,2},{4,5},{5,4},{6,7},{7,6},{8,9},{9,8},{10,11... | collective-permute-start | bytes 196616 | tf_op jit(solution)/shard_map/ppermute | solution.py:165
  5.3 2.2 %collective-permute-done = bf16[2,64,256]{2,1,0:T(8,128)(2,1)S(1)} collective-permute-done((bf16[2,64,256]{2,1,0:T(8,128)(2,1)S(1)}, bf16[2,64,256]{2,1,0:T(8,128)(2,1)S(1)}, u32[]{:S(2)}, u32[]{:S(2)}) %collective-permute-start) | collective-permute-done | bytes 65568 | tf_op jit(solution)/shard_map/ppermute | solution.py:165
  7.6 2.0 %collective-permute-start.1 = (bf16[1,2,64,256]{3,2,1,0:T(8,128)(2,1)S(1)}, bf16[1,2,64,256]{3,2,1,0:T(8,128)(2,1)S(1)}, u32[]{:S(2)}, u32[]{:S(2)}) collective-permute-start(bf16[1,2,64,256]{3,2,1,0:T(8,128)(2,1)S(1)} %get-tuple-element.13), channel_id=1, source_target_pairs={{0,8},{1,9},{2,10},{3,11},{4,20},{5,21},{6,22},{7,23},{8,0},{9,1},... | collective-permute-start | bytes 196616 | tf_op jit(solution)/shard_map/ppermute | solution.py:165
  9.6 2.6 %collective-permute-start.3 = (f32[2,64,256]{2,1,0:T(8,128)S(1)}, f32[2,64,256]{2,1,0:T(8,128)S(1)}, u32[]{:S(2)}, u32[]{:S(2)}) collective-permute-start(f32[2,64,256]{2,1,0:T(8,128)S(1)} %get-tuple-element.14.own_ref), channel_id=1, source_target_pairs={{0,2},{1,3},{2,0},{3,1},{4,6},{5,7},{6,4},{7,5},{8,10},{9,11},{10,... | collective-permute-start | bytes 393224 | tf_op jit(solution)/shard_map/ppermute | solution.py:165
  12.1 0.0 collective-permute-done.1
  12.2 0.1 collective-permute-start.2
  12.2 1.8 %collective-permute-start.4 = (bf16[2,2,64,256]{3,2,1,0:T(8,128)(2,1)S(1)}, bf16[2,2,64,256]{3,2,1,0:T(8,128)(2,1)S(1)}, u32[]{:S(2)}, u32[]{:S(2)}) collective-permute-start(bf16[2,2,64,256]{3,2,1,0:T(8,128)(2,1)S(1)} %pad_maximum_fusion.refs_0_), channel_id=1, source_target_pairs={{0,4},{1,5},{2,6},{3,7},{4,0},{5,1},{6,2},{7,3},{8,12},{9,13},{10,... | collective-permute-start | bytes 393224 | tf_op jit(solution)/shard_map/ppermute | solution.py:165
  14.0 3.1 %collective-permute-done.3.other_ref = f32[2,64,256]{2,1,0:T(8,128)S(1)} collective-permute-done((f32[2,64,256]{2,1,0:T(8,128)S(1)}, f32[2,64,256]{2,1,0:T(8,128)S(1)}, u32[]{:S(2)}, u32[]{:S(2)}) %collective-permute-start.3) | collective-permute-done | bytes 131104 | tf_op jit(solution)/shard_map/ppermute | solution.py:165
  17.1 0.0 collective-permute-done.2.refs_1_
  17.1 0.0 collective-permute-start.5
  17.1 0.0 copy-done
  17.1 0.8 %mix.1.mixed_ref = f32[8,2,64,256]{3,2,1,0:T(8,128)S(1)} custom-call(f32[2,64,256]{2,1,0:T(8,128)S(1)} %get-tuple-element.14.own_ref, f32[2,64,256]{2,1,0:T(8,128)S(1)} %collective-permute-done.3.other_ref, bf16[1,8,2,256,256]{4,3,2,1,0:T(8,128)(2,1)S(1)} %copy-done), custom_call_target="tpu_custom_call" | custom-call | flops 268435456 | bytes 262144 | tf_op jit(solution)/shard_map/mix/pallas_call | solution.py:89
  17.9 0.0 collective-permute-done.4.refs_2_
  17.9 0.5 %collective-permute-done.5.refs_3_ = bf16[2,2,64,256]{3,2,1,0:T(8,128)(2,1)S(1)} collective-permute-done((bf16[2,2,64,256]{3,2,1,0:T(8,128)(2,1)S(1)}, bf16[2,2,64,256]{3,2,1,0:T(8,128)(2,1)S(1)}, u32[]{:S(2)}, u32[]{:S(2)}) %collective-permute-start.5) | collective-permute-done | bytes 131104 | tf_op jit(solution)/shard_map/ppermute | solution.py:165
  18.5 0.0 copy-done.1
  18.5 0.0 copy-done.2
  18.5 0.6 %trace.1 = f32[2,16]{1,0:T(2,128)S(1)} custom-call(s32[1,16]{1,0:T(1,128)S(1)} %copy-done.1, s32[1,16]{1,0:T(1,128)S(1)} %copy-done.2, f32[8,2,64,256]{3,2,1,0:T(8,128)S(1)} %mix.1.mixed_ref, bf16[2,2,64,256]{3,2,1,0:T(8,128)(2,1)S(1)} %pad_maximum_fusion.refs_0_, bf16[2,2,64,256]{3,2,1,0:T(8,128)(2,1)S(1)} %collective-permute-done.2.refs_1_, ...), custom_call_target="tpu_custom_call" | custom-call | tf_op jit(solution)/shard_map/trace/pallas_call | solution.py:139
  19.1 1.0 %collective-permute-start.6 = (f32[2,16]{1,0:T(2,128)S(1)}, f32[2,16]{1,0:T(2,128)S(1)}, u32[]{:S(2)}, u32[]{:S(2)}) collective-permute-start(f32[2,16]{1,0:T(2,128)S(1)} %trace.1), channel_id=1, source_target_pairs={{0,5},{1,4},{2,7},{3,6},{4,1},{5,0},{6,3},{7,2},{8,13},{9,12},{10,... | collective-permute-start | bytes 392 | tf_op jit(solution)/shard_map/ppermute | solution.py:165
  20.1 0.4 %collective-permute-start.7 = (f32[2,16]{1,0:T(2,128)S(1)}, f32[2,16]{1,0:T(2,128)S(1)}, u32[]{:S(2)}, u32[]{:S(2)}) collective-permute-start(f32[2,16]{1,0:T(2,128)S(1)} %trace.1), channel_id=1, source_target_pairs={{0,4},{1,5},{2,6},{3,7},{4,0},{5,1},{6,2},{7,3},{8,12},{9,13},{10,... | collective-permute-start | bytes 392 | tf_op jit(solution)/shard_map/ppermute | solution.py:165
  20.4 1.6 %collective-permute-done.6 = f32[2,16]{1,0:T(2,128)S(1)} collective-permute-done((f32[2,16]{1,0:T(2,128)S(1)}, f32[2,16]{1,0:T(2,128)S(1)}, u32[]{:S(2)}, u32[]{:S(2)}) %collective-permute-start.6) | collective-permute-done | bytes 160 | tf_op jit(solution)/shard_map/ppermute | solution.py:165
  22.1 0.0 collective-permute-done.7
  22.1 2.0 %collective-permute-start.8 = (f32[2,16]{1,0:T(2,128)S(1)}, f32[2,16]{1,0:T(2,128)S(1)}, u32[]{:S(2)}, u32[]{:S(2)}) collective-permute-start(f32[2,16]{1,0:T(2,128)S(1)} %add.10), channel_id=1, source_target_pairs={{0,6},{1,7},{2,4},{3,5},{4,2},{5,3},{6,0},{7,1},{8,14},{9,15},{10,... | collective-permute-start | bytes 392 | tf_op jit(solution)/shard_map/ppermute | solution.py:165
  24.1 0.4 %collective-permute-start.9 = (f32[2,16]{1,0:T(2,128)S(1)}, f32[2,16]{1,0:T(2,128)S(1)}, u32[]{:S(2)}, u32[]{:S(2)}) collective-permute-start(f32[2,16]{1,0:T(2,128)S(1)} %add.10), channel_id=1, source_target_pairs={{0,4},{1,5},{2,6},{3,7},{4,0},{5,1},{6,2},{7,3},{8,12},{9,13},{10,... | collective-permute-start | bytes 392 | tf_op jit(solution)/shard_map/ppermute | solution.py:165
  24.5 1.5 %collective-permute-done.8 = f32[2,16]{1,0:T(2,128)S(1)} collective-permute-done((f32[2,16]{1,0:T(2,128)S(1)}, f32[2,16]{1,0:T(2,128)S(1)}, u32[]{:S(2)}, u32[]{:S(2)}) %collective-permute-start.8) | collective-permute-done | bytes 160 | tf_op jit(solution)/shard_map/ppermute | solution.py:165
  26.0 0.0 collective-permute-done.9
  26.0 0.6 %add.11 = f32[2,16]{1,0:T(2,128)} add(f32[2,16]{1,0:T(2,128)S(1)} %collective-permute-done.8, f32[2,16]{1,0:T(2,128)S(1)} %collective-permute-done.9) | non-fusion elementwise | flops 32 | bytes 384 | tf_op jit(solution)/shard_map/add | solution.py:190
  (3 shorter events, 0.0 us)
Async XLA Ops:
  0.0 17.1 %copy-start = (bf16[1,8,2,256,256]{4,3,2,1,0:T(8,128)(2,1)S(1)}, bf16[1,8,2,256,256]{4,3,2,1,0:T(8,128)(2,1)}, u32[]{:S(2)}) copy-start(bf16[1,8,2,256,256]{4,3,2,1,0:T(8,128)(2,1)} %elem_ref.1) | copy-start | bytes 6291460
  2.2 16.3 %copy-start.1 = (s32[1,16]{1,0:T(1,128)S(1)}, s32[1,16]{1,0:T(1,128)}, u32[]{:S(2)}) copy-start(s32[1,16]{1,0:T(1,128)} %sink_ref.1) | copy-start | bytes 196
  2.2 16.3 %copy-start.2 = (s32[1,16]{1,0:T(1,128)S(1)}, s32[1,16]{1,0:T(1,128)}, u32[]{:S(2)}) copy-start(s32[1,16]{1,0:T(1,128)} %mom_ref.1) | copy-start | bytes 196
  2.2 5.3 %collective-permute-start = (bf16[2,64,256]{2,1,0:T(8,128)(2,1)S(1)}, bf16[2,64,256]{2,1,0:T(8,128)(2,1)S(1)}, u32[]{:S(2)}, u32[]{:S(2)}) collective-permute-start(bf16[2,64,256]{2,1,0:T(8,128)(2,1)S(1)} %get-tuple-element.10), channel_id=1, source_target_pairs={{0,1},{1,0},{2,3},{3,2},{4,5},{5,4},{6,7},{7,6},{8,9},{9,8},{10,11... | collective-permute-start | bytes 196616 | tf_op jit(solution)/shard_map/ppermute | solution.py:165
  7.6 4.6 %collective-permute-start.1 = (bf16[1,2,64,256]{3,2,1,0:T(8,128)(2,1)S(1)}, bf16[1,2,64,256]{3,2,1,0:T(8,128)(2,1)S(1)}, u32[]{:S(2)}, u32[]{:S(2)}) collective-permute-start(bf16[1,2,64,256]{3,2,1,0:T(8,128)(2,1)S(1)} %get-tuple-element.13), channel_id=1, source_target_pairs={{0,8},{1,9},{2,10},{3,11},{4,20},{5,21},{6,22},{7,23},{8,0},{9,1},... | collective-permute-start | bytes 196616 | tf_op jit(solution)/shard_map/ppermute | solution.py:165
  9.6 7.5 %collective-permute-start.3 = (f32[2,64,256]{2,1,0:T(8,128)S(1)}, f32[2,64,256]{2,1,0:T(8,128)S(1)}, u32[]{:S(2)}, u32[]{:S(2)}) collective-permute-start(f32[2,64,256]{2,1,0:T(8,128)S(1)} %get-tuple-element.14.own_ref), channel_id=1, source_target_pairs={{0,2},{1,3},{2,0},{3,1},{4,6},{5,7},{6,4},{7,5},{8,10},{9,11},{10,... | collective-permute-start | bytes 393224 | tf_op jit(solution)/shard_map/ppermute | solution.py:165
  12.2 4.9 %collective-permute-start.2 = (bf16[2,2,64,256]{3,2,1,0:T(8,128)(2,1)S(1)}, bf16[2,2,64,256]{3,2,1,0:T(8,128)(2,1)S(1)}, u32[]{:S(2)}, u32[]{:S(2)}) collective-permute-start(bf16[2,2,64,256]{3,2,1,0:T(8,128)(2,1)S(1)} %pad_maximum_fusion.refs_0_), channel_id=1, source_target_pairs={{0,20},{1,21},{2,22},{3,23},{4,8},{5,9},{6,10},{7,11},{8,28},{9,29... | collective-permute-start | bytes 393224 | tf_op jit(solution)/shard_map/ppermute | solution.py:165
  12.2 5.7 %collective-permute-start.4 = (bf16[2,2,64,256]{3,2,1,0:T(8,128)(2,1)S(1)}, bf16[2,2,64,256]{3,2,1,0:T(8,128)(2,1)S(1)}, u32[]{:S(2)}, u32[]{:S(2)}) collective-permute-start(bf16[2,2,64,256]{3,2,1,0:T(8,128)(2,1)S(1)} %pad_maximum_fusion.refs_0_), channel_id=1, source_target_pairs={{0,4},{1,5},{2,6},{3,7},{4,0},{5,1},{6,2},{7,3},{8,12},{9,13},{10,... | collective-permute-start | bytes 393224 | tf_op jit(solution)/shard_map/ppermute | solution.py:165
  17.1 1.3 %collective-permute-start.5 = (bf16[2,2,64,256]{3,2,1,0:T(8,128)(2,1)S(1)}, bf16[2,2,64,256]{3,2,1,0:T(8,128)(2,1)S(1)}, u32[]{:S(2)}, u32[]{:S(2)}) collective-permute-start(bf16[2,2,64,256]{3,2,1,0:T(8,128)(2,1)S(1)} %collective-permute-done.2.refs_1_), channel_id=1, source_target_pairs={{0,4},{1,5},{2,6},{3,7},{4,0},{5,1},{6,2},{7,3},{8,12},{9,13},{10,... | collective-permute-start | bytes 393224 | tf_op jit(solution)/shard_map/ppermute | solution.py:165
  19.1 3.0 %collective-permute-start.6 = (f32[2,16]{1,0:T(2,128)S(1)}, f32[2,16]{1,0:T(2,128)S(1)}, u32[]{:S(2)}, u32[]{:S(2)}) collective-permute-start(f32[2,16]{1,0:T(2,128)S(1)} %trace.1), channel_id=1, source_target_pairs={{0,5},{1,4},{2,7},{3,6},{4,1},{5,0},{6,3},{7,2},{8,13},{9,12},{10,... | collective-permute-start | bytes 392 | tf_op jit(solution)/shard_map/ppermute | solution.py:165
  20.1 2.0 %collective-permute-start.7 = (f32[2,16]{1,0:T(2,128)S(1)}, f32[2,16]{1,0:T(2,128)S(1)}, u32[]{:S(2)}, u32[]{:S(2)}) collective-permute-start(f32[2,16]{1,0:T(2,128)S(1)} %trace.1), channel_id=1, source_target_pairs={{0,4},{1,5},{2,6},{3,7},{4,0},{5,1},{6,2},{7,3},{8,12},{9,13},{10,... | collective-permute-start | bytes 392 | tf_op jit(solution)/shard_map/ppermute | solution.py:165
  22.1 3.9 %collective-permute-start.8 = (f32[2,16]{1,0:T(2,128)S(1)}, f32[2,16]{1,0:T(2,128)S(1)}, u32[]{:S(2)}, u32[]{:S(2)}) collective-permute-start(f32[2,16]{1,0:T(2,128)S(1)} %add.10), channel_id=1, source_target_pairs={{0,6},{1,7},{2,4},{3,5},{4,2},{5,3},{6,0},{7,1},{8,14},{9,15},{10,... | collective-permute-start | bytes 392 | tf_op jit(solution)/shard_map/ppermute | solution.py:165
  24.1 1.9 %collective-permute-start.9 = (f32[2,16]{1,0:T(2,128)S(1)}, f32[2,16]{1,0:T(2,128)S(1)}, u32[]{:S(2)}, u32[]{:S(2)}) collective-permute-start(f32[2,16]{1,0:T(2,128)S(1)} %add.10), channel_id=1, source_target_pairs={{0,4},{1,5},{2,6},{3,7},{4,0},{5,1},{6,2},{7,3},{8,12},{9,13},{10,... | collective-permute-start | bytes 392 | tf_op jit(solution)/shard_map/ppermute | solution.py:165

commit v6 on v5

--- a/solution.py
+++ b/solution.py
@@ -70,8 +70,11 @@
 def mix_kernel(own_ref, other_ref, elem_ref, mixed_ref):
     momenta = elem_ref.shape[1]
     half = own_ref.shape[1]
-    full = (own_ref[...] + other_ref[...]).astype(jnp.bfloat16)
-    both = full.reshape(2 * half, full.shape[-1])
+    full = own_ref[...] + other_ref[...].astype(jnp.float32)
+    full = full.reshape(2 * half, full.shape[-1])
+    high = full.astype(jnp.bfloat16)
+    low = (full - high.astype(jnp.float32)).astype(jnp.bfloat16)
+    both = jnp.concatenate([high, low], axis=0)
     for p in range(momenta):
         by_real, by_imag = (
             lax.dot_general(
@@ -79,6 +82,8 @@
             )
             for r in range(2)
         )
+        by_real = by_real[: 2 * half] + by_real[2 * half :]
+        by_imag = by_imag[: 2 * half] + by_imag[2 * half :]
         mixed_ref[p, 0] = by_real[:half] - by_imag[half:]
         mixed_ref[p, 1] = by_imag[:half] + by_real[half:]
 
@@ -170,20 +175,18 @@
     keep, send = project(eigvecs, propagator)
     own = keep + across(send, 0).astype(jnp.float32)
     blocks = own.astype(jnp.bfloat16)[None]
-    total, other = own, jnp.zeros_like(own)
-    for bit in range(1, space_bits):
-        if bit > 1:
-            total = total + other
-        other = across(total, bit)
+    other = across(blocks[0], 1)
     for step in range(slice_bits - 1):
         flip = 1 if step == slice_bits - 2 else 0
         arrived = exchange(blocks, lambda t, s: (t ^ (1 << orders[t & 1][step]) ^ flip, s))
         if step < slice_bits - 2:
             blocks = jnp.concatenate([blocks, arrived], axis=0)
-    arrived, other = lax.optimization_barrier((arrived, other))
     cross = lambda t, s: (t ^ 1, s)
-    groups = [blocks, arrived, exchange(blocks, cross), exchange(arrived, cross)]
-    mixed = mix(total, other, elementals)
+    blocks_late, other = lax.optimization_barrier((blocks, other))
+    swapped = exchange(blocks_late, cross)
+    arrived, swapped = lax.optimization_barrier((arrived, swapped))
+    groups = [blocks, arrived, swapped, exchange(arrived, cross)]
+    mixed = mix(own, other, elementals)
     partial = trace(orders, sink_times, momenta, mixed, groups)
     for bit in range(space_bits):
         far = exchange(partial, lambda t, s: (t ^ 1, s ^ (1 << bit)))
@@ -240,7 +243,7 @@
     slice_bits, space_bits = slice_count.bit_length() - 1, space_count.bit_length() - 1
     on_device = by_collectives
     if (slice_count, space_count) == (1 << slice_bits, 1 << space_bits):
-        if slice_bits > 2 and space_bits > 0 and space_bits % 2 == 0:
+        if slice_bits > 2 and space_bits == 2:
             on_device = functools.partial(by_exchanges, slice_count, space_count)
     return jax.shard_map(
         on_device,

time: 26.7 us -> 26.2 us (0.981)
  starting transfers between devices: 13.3 us -> 12.6 us
  waiting for transfers between devices: 8.97 us -> 9.24 us
    ppermute x10, starting transfers between devices: 13.3 us -> 12.6 us  [exchange(): return lax.ppermute(value, axes, pairs)]
  transfers between devices with their start and end apart: 10 -> 10, of which waited for: 5 -> 6; matrix products, arithmetic and copies ran while one was open for 0% -> 0% of each run, Pallas kernels for 3% -> 3%
where the time goes in v6:
time: 26.2 us; the launch traced here: 26 us
  starting transfers between devices  12.6 us (48%)
  waiting for transfers between devices  9.24 us (35%)
  Pallas kernels  3.51 us (13%)
  other arithmetic  0.6 us (2%)
    ppermute x10, starting transfers between devices, exchange(): return lax.ppermute(value, axes, pairs)  12.6 us
    ppermute x10, waiting for transfers between devices, exchange(): return lax.ppermute(value, axes, pairs)  9.24 us
    pallas_call x1, Pallas kernels, project(): pl.pallas_call(project_kernel, out_shape=(jax.ShapeDtypeStruct(shape, jnp...  2.16 us
    pallas_call x1, Pallas kernels, mix(): pl.pallas_call(mix_kernel, out_shape=jax.ShapeDtypeStruct((momenta,) + ow...  0.74 us
    pallas_call x1, Pallas kernels, trace(): pl.pallas_call(functools.partial(trace_kernel, orders), out_shape=jax.Sha...  0.61 us
    add x2, other arithmetic, by_exchanges(): partial = far + exchange(partial, cross)  0.57 us
  transfers between devices with their start and end apart: 10, of which 6 were waited for; matrix products, arithmetic and copies ran while one was open for 0% of the time, Pallas kernels for 3%

profile of v6, /device:TPU:0, one launch (start us, length us, event | category | flops | bytes accessed | tf_op | source)
XLA Modules:
  0.0 26.0 jit_solution(6732023581067181246)
XLA Ops:
  0.0 0.0 copy-start
  0.0 2.2 %project.1 = (f32[2,64,256]{2,1,0:T(8,128)S(1)}, bf16[2,64,256]{2,1,0:T(8,128)(2,1)S(1)}) custom-call(bf16[2,3,1,512,256]{4,3,2,1,0:T(8,128)(2,1)} %vec_hbm.1, bf16[2,3,1,512,128]{4,3,2,1,0:T(8,128)(2,1)} %prop_hbm.1), custom_call_target="tpu_custom_call" | custom-call | tf_op jit(solution)/shard_map/project/pallas_call | solution.py:51
  2.2 0.0 copy-start.1
  2.2 0.0 copy-start.2
  2.2 3.1 %collective-permute-start = (bf16[2,64,256]{2,1,0:T(8,128)(2,1)S(1)}, bf16[2,64,256]{2,1,0:T(8,128)(2,1)S(1)}, u32[]{:S(2)}, u32[]{:S(2)}) collective-permute-start(bf16[2,64,256]{2,1,0:T(8,128)(2,1)S(1)} %get-tuple-element.12), channel_id=1, source_target_pairs={{0,1},{1,0},{2,3},{3,2},{4,5},{5,4},{6,7},{7,6},{8,9},{9,8},{10,11... | collective-permute-start | bytes 196616 | tf_op jit(solution)/shard_map/ppermute | solution.py:170
  5.3 2.2 %collective-permute-done = bf16[2,64,256]{2,1,0:T(8,128)(2,1)S(1)} collective-permute-done((bf16[2,64,256]{2,1,0:T(8,128)(2,1)S(1)}, bf16[2,64,256]{2,1,0:T(8,128)(2,1)S(1)}, u32[]{:S(2)}, u32[]{:S(2)}) %collective-permute-start) | collective-permute-done | bytes 65568 | tf_op jit(solution)/shard_map/ppermute | solution.py:170
  7.6 2.0 %collective-permute-start.1 = (bf16[1,2,64,256]{3,2,1,0:T(8,128)(2,1)S(1)}, bf16[1,2,64,256]{3,2,1,0:T(8,128)(2,1)S(1)}, u32[]{:S(2)}, u32[]{:S(2)}) collective-permute-start(bf16[1,2,64,256]{3,2,1,0:T(8,128)(2,1)S(1)} %bitcast.4), channel_id=1, source_target_pairs={{0,8},{1,9},{2,10},{3,11},{4,20},{5,21},{6,22},{7,23},{8,0},{9,1},... | collective-permute-start | bytes 196616 | tf_op jit(solution)/shard_map/ppermute | solution.py:170
  9.6 2.6 %collective-permute-start.2 = (bf16[2,64,256]{2,1,0:T(8,128)(2,1)S(1)}, bf16[2,64,256]{2,1,0:T(8,128)(2,1)S(1)}, u32[]{:S(2)}, u32[]{:S(2)}) collective-permute-start(bf16[2,64,256]{2,1,0:T(8,128)(2,1)S(1)} %get-tuple-element.17), channel_id=1, source_target_pairs={{0,2},{1,3},{2,0},{3,1},{4,6},{5,7},{6,4},{7,5},{8,10},{9,11},{10,... | collective-permute-start | bytes 196616 | tf_op jit(solution)/shard_map/ppermute | solution.py:170
  12.1 0.0 collective-permute-done.1
  12.2 0.1 collective-permute-start.3
  12.2 2.5 %collective-permute-done.2.other_ref = bf16[2,64,256]{2,1,0:T(8,128)(2,1)S(1)} collective-permute-done((bf16[2,64,256]{2,1,0:T(8,128)(2,1)S(1)}, bf16[2,64,256]{2,1,0:T(8,128)(2,1)S(1)}, u32[]{:S(2)}, u32[]{:S(2)}) %collective-permute-start.2) | collective-permute-done | bytes 65568 | tf_op jit(solution)/shard_map/ppermute | solution.py:170
  14.7 0.0 collective-permute-start.4
  14.7 1.9 %collective-permute-done.3.refs_1_ = bf16[2,2,64,256]{3,2,1,0:T(8,128)(2,1)S(1)} collective-permute-done((bf16[2,2,64,256]{3,2,1,0:T(8,128)(2,1)S(1)}, bf16[2,2,64,256]{3,2,1,0:T(8,128)(2,1)S(1)}, u32[]{:S(2)}, u32[]{:S(2)}) %collective-permute-start.3) | collective-permute-done | bytes 131104 | tf_op jit(solution)/shard_map/ppermute | solution.py:170
  16.6 0.0 collective-permute-done.4.refs_2_
  16.6 0.1 collective-permute-start.5
  16.7 0.0 copy-done
  16.7 0.7 %mix.1.mixed_ref = f32[8,2,64,256]{3,2,1,0:T(8,128)S(1)} custom-call(f32[2,64,256]{2,1,0:T(8,128)S(1)} %get-tuple-element.18.own_ref, bf16[2,64,256]{2,1,0:T(8,128)(2,1)S(1)} %collective-permute-done.2.other_ref, bf16[1,8,2,256,256]{4,3,2,1,0:T(8,128)(2,1)S(1)} %copy-done), custom_call_target="tpu_custom_call" | custom-call | flops 268435456 | bytes 262144 | tf_op jit(solution)/shard_map/mix/pallas_call | solution.py:94
  17.5 0.5 %collective-permute-done.5.refs_3_ = bf16[2,2,64,256]{3,2,1,0:T(8,128)(2,1)S(1)} collective-permute-done((bf16[2,2,64,256]{3,2,1,0:T(8,128)(2,1)S(1)}, bf16[2,2,64,256]{3,2,1,0:T(8,128)(2,1)S(1)}, u32[]{:S(2)}, u32[]{:S(2)}) %collective-permute-start.5) | collective-permute-done | bytes 131104 | tf_op jit(solution)/shard_map/ppermute | solution.py:170
  18.0 0.0 copy-done.1
  18.0 0.0 copy-done.2
  18.0 0.6 %trace.1 = f32[2,16]{1,0:T(2,128)S(1)} custom-call(s32[1,16]{1,0:T(1,128)S(1)} %copy-done.1, s32[1,16]{1,0:T(1,128)S(1)} %copy-done.2, f32[8,2,64,256]{3,2,1,0:T(8,128)S(1)} %mix.1.mixed_ref, bf16[2,2,64,256]{3,2,1,0:T(8,128)(2,1)S(1)} %pad_maximum_fusion.refs_0_, bf16[2,2,64,256]{3,2,1,0:T(8,128)(2,1)S(1)} %collective-permute-done.3.refs_1_, ...), custom_call_target="tpu_custom_call" | custom-call | tf_op jit(solution)/shard_map/trace/pallas_call | solution.py:144
  18.6 1.5 %collective-permute-start.6 = (f32[2,16]{1,0:T(2,128)S(1)}, f32[2,16]{1,0:T(2,128)S(1)}, u32[]{:S(2)}, u32[]{:S(2)}) collective-permute-start(f32[2,16]{1,0:T(2,128)S(1)} %trace.1), channel_id=1, source_target_pairs={{0,5},{1,4},{2,7},{3,6},{4,1},{5,0},{6,3},{7,2},{8,13},{9,12},{10,... | collective-permute-start | bytes 392 | tf_op jit(solution)/shard_map/ppermute | solution.py:170
  20.1 0.4 %collective-permute-start.7 = (f32[2,16]{1,0:T(2,128)S(1)}, f32[2,16]{1,0:T(2,128)S(1)}, u32[]{:S(2)}, u32[]{:S(2)}) collective-permute-start(f32[2,16]{1,0:T(2,128)S(1)} %trace.1), channel_id=1, source_target_pairs={{0,4},{1,5},{2,6},{3,7},{4,0},{5,1},{6,2},{7,3},{8,12},{9,13},{10,... | collective-permute-start | bytes 392 | tf_op jit(solution)/shard_map/ppermute | solution.py:170
  20.5 1.1 %collective-permute-done.6 = f32[2,16]{1,0:T(2,128)S(1)} collective-permute-done((f32[2,16]{1,0:T(2,128)S(1)}, f32[2,16]{1,0:T(2,128)S(1)}, u32[]{:S(2)}, u32[]{:S(2)}) %collective-permute-start.6) | collective-permute-done | bytes 160 | tf_op jit(solution)/shard_map/ppermute | solution.py:170
  21.6 0.0 collective-permute-done.7
  21.6 2.5 %collective-permute-start.8 = (f32[2,16]{1,0:T(2,128)S(1)}, f32[2,16]{1,0:T(2,128)S(1)}, u32[]{:S(2)}, u32[]{:S(2)}) collective-permute-start(f32[2,16]{1,0:T(2,128)S(1)} %add.10), channel_id=1, source_target_pairs={{0,6},{1,7},{2,4},{3,5},{4,2},{5,3},{6,0},{7,1},{8,14},{9,15},{10,... | collective-permute-start | bytes 392 | tf_op jit(solution)/shard_map/ppermute | solution.py:170
  24.1 0.4 %collective-permute-start.9 = (f32[2,16]{1,0:T(2,128)S(1)}, f32[2,16]{1,0:T(2,128)S(1)}, u32[]{:S(2)}, u32[]{:S(2)}) collective-permute-start(f32[2,16]{1,0:T(2,128)S(1)} %add.10), channel_id=1, source_target_pairs={{0,4},{1,5},{2,6},{3,7},{4,0},{5,1},{6,2},{7,3},{8,12},{9,13},{10,... | collective-permute-start | bytes 392 | tf_op jit(solution)/shard_map/ppermute | solution.py:170
  24.5 1.0 %collective-permute-done.8 = f32[2,16]{1,0:T(2,128)S(1)} collective-permute-done((f32[2,16]{1,0:T(2,128)S(1)}, f32[2,16]{1,0:T(2,128)S(1)}, u32[]{:S(2)}, u32[]{:S(2)}) %collective-permute-start.8) | collective-permute-done | bytes 160 | tf_op jit(solution)/shard_map/ppermute | solution.py:170
  25.5 0.0 collective-permute-done.9
  25.5 0.6 %add.11 = f32[2,16]{1,0:T(2,128)} add(f32[2,16]{1,0:T(2,128)S(1)} %collective-permute-done.8, f32[2,16]{1,0:T(2,128)S(1)} %collective-permute-done.9) | non-fusion elementwise | flops 32 | bytes 384 | tf_op jit(solution)/shard_map/add | solution.py:193
  (3 shorter events, 0.0 us)
Async XLA Ops:
  0.0 16.7 %copy-start = (bf16[1,8,2,256,256]{4,3,2,1,0:T(8,128)(2,1)S(1)}, bf16[1,8,2,256,256]{4,3,2,1,0:T(8,128)(2,1)}, u32[]{:S(2)}) copy-start(bf16[1,8,2,256,256]{4,3,2,1,0:T(8,128)(2,1)} %elem_ref.1) | copy-start | bytes 6291460
  2.2 15.8 %copy-start.1 = (s32[1,16]{1,0:T(1,128)S(1)}, s32[1,16]{1,0:T(1,128)}, u32[]{:S(2)}) copy-start(s32[1,16]{1,0:T(1,128)} %sink_ref.1) | copy-start | bytes 196
  2.2 15.8 %copy-start.2 = (s32[1,16]{1,0:T(1,128)S(1)}, s32[1,16]{1,0:T(1,128)}, u32[]{:S(2)}) copy-start(s32[1,16]{1,0:T(1,128)} %mom_ref.1) | copy-start | bytes 196
  2.2 5.3 %collective-permute-start = (bf16[2,64,256]{2,1,0:T(8,128)(2,1)S(1)}, bf16[2,64,256]{2,1,0:T(8,128)(2,1)S(1)}, u32[]{:S(2)}, u32[]{:S(2)}) collective-permute-start(bf16[2,64,256]{2,1,0:T(8,128)(2,1)S(1)} %get-tuple-element.12), channel_id=1, source_target_pairs={{0,1},{1,0},{2,3},{3,2},{4,5},{5,4},{6,7},{7,6},{8,9},{9,8},{10,11... | collective-permute-start | bytes 196616 | tf_op jit(solution)/shard_map/ppermute | solution.py:170
  7.6 4.6 %collective-permute-start.1 = (bf16[1,2,64,256]{3,2,1,0:T(8,128)(2,1)S(1)}, bf16[1,2,64,256]{3,2,1,0:T(8,128)(2,1)S(1)}, u32[]{:S(2)}, u32[]{:S(2)}) collective-permute-start(bf16[1,2,64,256]{3,2,1,0:T(8,128)(2,1)S(1)} %bitcast.4), channel_id=1, source_target_pairs={{0,8},{1,9},{2,10},{3,11},{4,20},{5,21},{6,22},{7,23},{8,0},{9,1},... | collective-permute-start | bytes 196616 | tf_op jit(solution)/shard_map/ppermute | solution.py:170
  9.6 5.2 %collective-permute-start.2 = (bf16[2,64,256]{2,1,0:T(8,128)(2,1)S(1)}, bf16[2,64,256]{2,1,0:T(8,128)(2,1)S(1)}, u32[]{:S(2)}, u32[]{:S(2)}) collective-permute-start(bf16[2,64,256]{2,1,0:T(8,128)(2,1)S(1)} %get-tuple-element.17), channel_id=1, source_target_pairs={{0,2},{1,3},{2,0},{3,1},{4,6},{5,7},{6,4},{7,5},{8,10},{9,11},{10,... | collective-permute-start | bytes 196616 | tf_op jit(solution)/shard_map/ppermute | solution.py:170
  12.2 4.4 %collective-permute-start.3 = (bf16[2,2,64,256]{3,2,1,0:T(8,128)(2,1)S(1)}, bf16[2,2,64,256]{3,2,1,0:T(8,128)(2,1)S(1)}, u32[]{:S(2)}, u32[]{:S(2)}) collective-permute-start(bf16[2,2,64,256]{3,2,1,0:T(8,128)(2,1)S(1)} %pad_maximum_fusion.refs_0_), channel_id=1, source_target_pairs={{0,20},{1,21},{2,22},{3,23},{4,8},{5,9},{6,10},{7,11},{8,28},{9,29... | collective-permute-start | bytes 393224 | tf_op jit(solution)/shard_map/ppermute | solution.py:170
  14.7 1.9 %collective-permute-start.4 = (bf16[2,2,64,256]{3,2,1,0:T(8,128)(2,1)S(1)}, bf16[2,2,64,256]{3,2,1,0:T(8,128)(2,1)S(1)}, u32[]{:S(2)}, u32[]{:S(2)}) collective-permute-start(bf16[2,2,64,256]{3,2,1,0:T(8,128)(2,1)S(1)} %pad_maximum_fusion.refs_0_), channel_id=1, source_target_pairs={{0,4},{1,5},{2,6},{3,7},{4,0},{5,1},{6,2},{7,3},{8,12},{9,13},{10,... | collective-permute-start | bytes 393224 | tf_op jit(solution)/shard_map/ppermute | solution.py:170
  16.6 1.3 %collective-permute-start.5 = (bf16[2,2,64,256]{3,2,1,0:T(8,128)(2,1)S(1)}, bf16[2,2,64,256]{3,2,1,0:T(8,128)(2,1)S(1)}, u32[]{:S(2)}, u32[]{:S(2)}) collective-permute-start(bf16[2,2,64,256]{3,2,1,0:T(8,128)(2,1)S(1)} %collective-permute-done.3.refs_1_), channel_id=1, source_target_pairs={{0,4},{1,5},{2,6},{3,7},{4,0},{5,1},{6,2},{7,3},{8,12},{9,13},{10,... | collective-permute-start | bytes 393224 | tf_op jit(solution)/shard_map/ppermute | solution.py:170
  18.6 3.0 %collective-permute-start.6 = (f32[2,16]{1,0:T(2,128)S(1)}, f32[2,16]{1,0:T(2,128)S(1)}, u32[]{:S(2)}, u32[]{:S(2)}) collective-permute-start(f32[2,16]{1,0:T(2,128)S(1)} %trace.1), channel_id=1, source_target_pairs={{0,5},{1,4},{2,7},{3,6},{4,1},{5,0},{6,3},{7,2},{8,13},{9,12},{10,... | collective-permute-start | bytes 392 | tf_op jit(solution)/shard_map/ppermute | solution.py:170
  20.1 1.5 %collective-permute-start.7 = (f32[2,16]{1,0:T(2,128)S(1)}, f32[2,16]{1,0:T(2,128)S(1)}, u32[]{:S(2)}, u32[]{:S(2)}) collective-permute-start(f32[2,16]{1,0:T(2,128)S(1)} %trace.1), channel_id=1, source_target_pairs={{0,4},{1,5},{2,6},{3,7},{4,0},{5,1},{6,2},{7,3},{8,12},{9,13},{10,... | collective-permute-start | bytes 392 | tf_op jit(solution)/shard_map/ppermute | solution.py:170
  21.6 3.9 %collective-permute-start.8 = (f32[2,16]{1,0:T(2,128)S(1)}, f32[2,16]{1,0:T(2,128)S(1)}, u32[]{:S(2)}, u32[]{:S(2)}) collective-permute-start(f32[2,16]{1,0:T(2,128)S(1)} %add.10), channel_id=1, source_target_pairs={{0,6},{1,7},{2,4},{3,5},{4,2},{5,3},{6,0},{7,1},{8,14},{9,15},{10,... | collective-permute-start | bytes 392 | tf_op jit(solution)/shard_map/ppermute | solution.py:170
  24.1 1.4 %collective-permute-start.9 = (f32[2,16]{1,0:T(2,128)S(1)}, f32[2,16]{1,0:T(2,128)S(1)}, u32[]{:S(2)}, u32[]{:S(2)}) collective-permute-start(f32[2,16]{1,0:T(2,128)S(1)} %add.10), channel_id=1, source_target_pairs={{0,4},{1,5},{2,6},{3,7},{4,0},{5,1},{6,2},{7,3},{8,12},{9,13},{10,... | collective-permute-start | bytes 392 | tf_op jit(solution)/shard_map/ppermute | solution.py:170

commit v7 on v6

--- a/solution.py
+++ b/solution.py
@@ -104,27 +104,14 @@
     )(own, other, elementals)
 
 
-def trace_kernel(orders, sink_ref, mom_ref, mixed_ref, *refs):
+def trace_kernel(slot_ref, mom_ref, mixed_ref, *refs):
     groups, out_ref, slices_ref, sums_ref = refs[:-3], refs[-3], refs[-2], refs[-1]
     items = out_ref.shape[1]
-    per_group = groups[0].shape[0]
-    own_slice = lax.axis_index("tm")
-    own_core = own_slice & 1
     for g, ref in enumerate(groups):
-        slices_ref[g * per_group : (g + 1) * per_group] = ref[...]
+        slices_ref[g * ref.shape[0] : (g + 1) * ref.shape[0]] = ref[...]
     for k in range(items):
         p = mom_ref[0, k]
-        away = sink_ref[0, k] ^ own_slice
-        crossed = away & 1
-        slots = []
-        for order in orders:
-            slot = 0
-            for place, bit in enumerate(order):
-                slot = slot + (((away >> bit) & 1) << place)
-            slots.append(slot)
-        slot = jnp.where(own_core ^ crossed == 0, slots[0], slots[1])
-        crossed = crossed ^ (slot >> (len(orders[0]) - 1))
-        slot = slot + crossed * (2 * per_group)
+        slot = slot_ref[0, k]
         real = slices_ref[slot, 0].astype(jnp.float32)
         imag = slices_ref[slot, 1].astype(jnp.float32)
         mixed_real = mixed_ref[p, 0]
@@ -138,11 +125,11 @@
     out_ref[...] = jnp.sum(jnp.sum(sums_ref[...], axis=2), axis=-1)
 
 
-def trace(orders, sink_times, momenta, mixed, groups):
-    items = sink_times.shape[1]
+def trace(slots, momenta, mixed, groups):
+    items = slots.shape[1]
     per_group = groups[0].shape[0]
     return pl.pallas_call(
-        functools.partial(trace_kernel, orders),
+        trace_kernel,
         out_shape=jax.ShapeDtypeStruct((2, items), jnp.float32),
         in_specs=[pl.BlockSpec(memory_space=pltpu.VMEM)] * (3 + len(groups)),
         out_specs=pl.BlockSpec(memory_space=pltpu.VMEM),
@@ -152,7 +139,22 @@
         ],
         compiler_params=pltpu.CompilerParams(vmem_limit_bytes=16 * MIB),
         name="trace",
-    )(sink_times, momenta, mixed, *groups)
+    )(slots, momenta, mixed, *groups)
+
+
+def slots_of(orders, sink_times):
+    own_slice = lax.axis_index("tm")
+    steps = len(orders[0])
+    away = sink_times ^ own_slice
+    by_core = []
+    for order in orders:
+        slot = jnp.zeros_like(away)
+        for place, bit in enumerate(order):
+            slot = slot + (((away >> bit) & 1) << place)
+        by_core.append(slot)
+    slot = jnp.where(sink_times & 1 == 0, by_core[0], by_core[1])
+    crossed = (away & 1) ^ (slot >> (steps - 1))
+    return slot + (crossed << steps)
 
 
 def by_exchanges(slice_count, space_count, eigvecs, propagator, elementals, sink_times, momenta):
@@ -187,7 +189,7 @@
     arrived, swapped = lax.optimization_barrier((arrived, swapped))
     groups = [blocks, arrived, swapped, exchange(arrived, cross)]
     mixed = mix(own, other, elementals)
-    partial = trace(orders, sink_times, momenta, mixed, groups)
+    partial = trace(slots_of(orders, sink_times), momenta, mixed, groups)
     for bit in range(space_bits):
         far = exchange(partial, lambda t, s: (t ^ 1, s ^ (1 << bit)))
         partial = far + exchange(partial, cross)

time: 26.2 us -> 26.2 us (level)
  no operation moved by 1% of the time
where the time goes in v7:
time: 26.2 us; the launch traced here: 26 us
  starting transfers between devices  12.6 us (48%)
  waiting for transfers between devices  9.22 us (35%)
  Pallas kernels  3.49 us (13%)
  other arithmetic  0.61 us (2%)
    ppermute x10, starting transfers between devices, exchange(): return lax.ppermute(value, axes, pairs)  12.6 us
    ppermute x10, waiting for transfers between devices, exchange(): return lax.ppermute(value, axes, pairs)  9.22 us
    pallas_call x1, Pallas kernels, project(): pl.pallas_call(project_kernel, out_shape=(jax.ShapeDtypeStruct(shape, jnp...  2.16 us
    pallas_call x1, Pallas kernels, mix(): pl.pallas_call(mix_kernel, out_shape=jax.ShapeDtypeStruct((momenta,) + ow...  0.74 us
    pallas_call x1, Pallas kernels, trace(): pl.pallas_call(trace_kernel, out_shape=jax.ShapeDtypeStruct((2, items), j...  0.59 us
    add x2, other arithmetic, by_exchanges(): partial = far + exchange(partial, cross)  0.57 us
  transfers between devices with their start and end apart: 10, of which 6 were waited for; matrix products, arithmetic and copies ran while one was open for 0% of the time, Pallas kernels for 3%

profile of v7, /device:TPU:0, one launch (start us, length us, event | category | flops | bytes accessed | tf_op | source)
XLA Modules:
  0.0 26.0 jit_solution(4211678954006451421)
XLA Ops:
  0.0 0.0 copy-start.2
  0.0 0.0 copy-start
  0.0 2.2 %project.1 = (f32[2,64,256]{2,1,0:T(8,128)S(1)}, bf16[2,64,256]{2,1,0:T(8,128)(2,1)S(1)}) custom-call(bf16[2,3,1,512,256]{4,3,2,1,0:T(8,128)(2,1)} %vec_hbm.1, bf16[2,3,1,512,128]{4,3,2,1,0:T(8,128)(2,1)} %prop_hbm.1), custom_call_target="tpu_custom_call" | custom-call | tf_op jit(solution)/shard_map/project/pallas_call | solution.py:51
  2.2 0.0 copy-start.1
  2.2 3.1 %collective-permute-start = (bf16[2,64,256]{2,1,0:T(8,128)(2,1)S(1)}, bf16[2,64,256]{2,1,0:T(8,128)(2,1)S(1)}, u32[]{:S(2)}, u32[]{:S(2)}) collective-permute-start(bf16[2,64,256]{2,1,0:T(8,128)(2,1)S(1)} %get-tuple-element.12), channel_id=1, source_target_pairs={{0,1},{1,0},{2,3},{3,2},{4,5},{5,4},{6,7},{7,6},{8,9},{9,8},{10,11... | collective-permute-start | bytes 196616 | tf_op jit(solution)/shard_map/ppermute | solution.py:172
  5.3 2.2 %collective-permute-done = bf16[2,64,256]{2,1,0:T(8,128)(2,1)S(1)} collective-permute-done((bf16[2,64,256]{2,1,0:T(8,128)(2,1)S(1)}, bf16[2,64,256]{2,1,0:T(8,128)(2,1)S(1)}, u32[]{:S(2)}, u32[]{:S(2)}) %collective-permute-start) | collective-permute-done | bytes 65568 | tf_op jit(solution)/shard_map/ppermute | solution.py:172
  7.5 2.0 %collective-permute-start.1 = (bf16[1,2,64,256]{3,2,1,0:T(8,128)(2,1)S(1)}, bf16[1,2,64,256]{3,2,1,0:T(8,128)(2,1)S(1)}, u32[]{:S(2)}, u32[]{:S(2)}) collective-permute-start(bf16[1,2,64,256]{3,2,1,0:T(8,128)(2,1)S(1)} %bitcast.4), channel_id=1, source_target_pairs={{0,8},{1,9},{2,10},{3,11},{4,20},{5,21},{6,22},{7,23},{8,0},{9,1},... | collective-permute-start | bytes 196616 | tf_op jit(solution)/shard_map/ppermute | solution.py:172
  9.5 2.6 %collective-permute-start.2 = (bf16[2,64,256]{2,1,0:T(8,128)(2,1)S(1)}, bf16[2,64,256]{2,1,0:T(8,128)(2,1)S(1)}, u32[]{:S(2)}, u32[]{:S(2)}) collective-permute-start(bf16[2,64,256]{2,1,0:T(8,128)(2,1)S(1)} %get-tuple-element.17), channel_id=1, source_target_pairs={{0,2},{1,3},{2,0},{3,1},{4,6},{5,7},{6,4},{7,5},{8,10},{9,11},{10,... | collective-permute-start | bytes 196616 | tf_op jit(solution)/shard_map/ppermute | solution.py:172
  12.1 0.0 collective-permute-done.1
  12.2 0.1 collective-permute-start.3
  12.2 2.5 %collective-permute-done.2.other_ref = bf16[2,64,256]{2,1,0:T(8,128)(2,1)S(1)} collective-permute-done((bf16[2,64,256]{2,1,0:T(8,128)(2,1)S(1)}, bf16[2,64,256]{2,1,0:T(8,128)(2,1)S(1)}, u32[]{:S(2)}, u32[]{:S(2)}) %collective-permute-start.2) | collective-permute-done | bytes 65568 | tf_op jit(solution)/shard_map/ppermute | solution.py:172
  14.7 0.0 collective-permute-start.4
  14.7 1.9 %collective-permute-done.3.refs_1_ = bf16[2,2,64,256]{3,2,1,0:T(8,128)(2,1)S(1)} collective-permute-done((bf16[2,2,64,256]{3,2,1,0:T(8,128)(2,1)S(1)}, bf16[2,2,64,256]{3,2,1,0:T(8,128)(2,1)S(1)}, u32[]{:S(2)}, u32[]{:S(2)}) %collective-permute-start.3) | collective-permute-done | bytes 131104 | tf_op jit(solution)/shard_map/ppermute | solution.py:172
  16.6 0.0 collective-permute-done.4.refs_2_
  16.6 0.1 collective-permute-start.5
  16.7 0.0 copy-done.2
  16.7 0.0 copy-done
  16.7 0.7 %mix.1.mixed_ref = f32[8,2,64,256]{3,2,1,0:T(8,128)S(1)} custom-call(f32[2,64,256]{2,1,0:T(8,128)S(1)} %get-tuple-element.18.own_ref, bf16[2,64,256]{2,1,0:T(8,128)(2,1)S(1)} %collective-permute-done.2.other_ref, bf16[1,8,2,256,256]{4,3,2,1,0:T(8,128)(2,1)S(1)} %copy-done), custom_call_target="tpu_custom_call" | custom-call | flops 268435456 | bytes 262144 | tf_op jit(solution)/shard_map/mix/pallas_call | solution.py:94
  17.5 0.5 %collective-permute-done.5.refs_3_ = bf16[2,2,64,256]{3,2,1,0:T(8,128)(2,1)S(1)} collective-permute-done((bf16[2,2,64,256]{3,2,1,0:T(8,128)(2,1)S(1)}, bf16[2,2,64,256]{3,2,1,0:T(8,128)(2,1)S(1)}, u32[]{:S(2)}, u32[]{:S(2)}) %collective-permute-start.5) | collective-permute-done | bytes 131104 | tf_op jit(solution)/shard_map/ppermute | solution.py:172
  18.0 0.0 copy-done.1
  18.0 0.6 %trace.1 = f32[2,16]{1,0:T(2,128)S(1)} custom-call(s32[1,16]{1,0:T(1,128)S(1)} %shift-left_add_fusion.slot_ref, s32[1,16]{1,0:T(1,128)S(1)} %copy-done.1, f32[8,2,64,256]{3,2,1,0:T(8,128)S(1)} %mix.1.mixed_ref, bf16[2,2,64,256]{3,2,1,0:T(8,128)(2,1)S(1)} %pad_maximum_fusion.refs_0_, bf16[2,2,64,256]{3,2,1,0:T(8,128)(2,1)S(1)} %collective-permute-done.3.refs_1_, ...), custom_call_target="tpu_custom_call" | custom-call | tf_op jit(solution)/shard_map/trace/pallas_call | solution.py:131
  18.5 1.5 %collective-permute-start.6 = (f32[2,16]{1,0:T(2,128)S(1)}, f32[2,16]{1,0:T(2,128)S(1)}, u32[]{:S(2)}, u32[]{:S(2)}) collective-permute-start(f32[2,16]{1,0:T(2,128)S(1)} %trace.1), channel_id=1, source_target_pairs={{0,5},{1,4},{2,7},{3,6},{4,1},{5,0},{6,3},{7,2},{8,13},{9,12},{10,... | collective-permute-start | bytes 392 | tf_op jit(solution)/shard_map/ppermute | solution.py:172
  20.1 0.4 %collective-permute-start.7 = (f32[2,16]{1,0:T(2,128)S(1)}, f32[2,16]{1,0:T(2,128)S(1)}, u32[]{:S(2)}, u32[]{:S(2)}) collective-permute-start(f32[2,16]{1,0:T(2,128)S(1)} %trace.1), channel_id=1, source_target_pairs={{0,4},{1,5},{2,6},{3,7},{4,0},{5,1},{6,2},{7,3},{8,12},{9,13},{10,... | collective-permute-start | bytes 392 | tf_op jit(solution)/shard_map/ppermute | solution.py:172
  20.4 1.1 %collective-permute-done.6 = f32[2,16]{1,0:T(2,128)S(1)} collective-permute-done((f32[2,16]{1,0:T(2,128)S(1)}, f32[2,16]{1,0:T(2,128)S(1)}, u32[]{:S(2)}, u32[]{:S(2)}) %collective-permute-start.6) | collective-permute-done | bytes 160 | tf_op jit(solution)/shard_map/ppermute | solution.py:172
  21.5 0.0 collective-permute-done.7
  21.5 2.5 %collective-permute-start.8 = (f32[2,16]{1,0:T(2,128)S(1)}, f32[2,16]{1,0:T(2,128)S(1)}, u32[]{:S(2)}, u32[]{:S(2)}) collective-permute-start(f32[2,16]{1,0:T(2,128)S(1)} %add.22), channel_id=1, source_target_pairs={{0,6},{1,7},{2,4},{3,5},{4,2},{5,3},{6,0},{7,1},{8,14},{9,15},{10,... | collective-permute-start | bytes 392 | tf_op jit(solution)/shard_map/ppermute | solution.py:172
  24.1 0.4 %collective-permute-start.9 = (f32[2,16]{1,0:T(2,128)S(1)}, f32[2,16]{1,0:T(2,128)S(1)}, u32[]{:S(2)}, u32[]{:S(2)}) collective-permute-start(f32[2,16]{1,0:T(2,128)S(1)} %add.22), channel_id=1, source_target_pairs={{0,4},{1,5},{2,6},{3,7},{4,0},{5,1},{6,2},{7,3},{8,12},{9,13},{10,... | collective-permute-start | bytes 392 | tf_op jit(solution)/shard_map/ppermute | solution.py:172
  24.4 1.0 %collective-permute-done.8 = f32[2,16]{1,0:T(2,128)S(1)} collective-permute-done((f32[2,16]{1,0:T(2,128)S(1)}, f32[2,16]{1,0:T(2,128)S(1)}, u32[]{:S(2)}, u32[]{:S(2)}) %collective-permute-start.8) | collective-permute-done | bytes 160 | tf_op jit(solution)/shard_map/ppermute | solution.py:172
  25.4 0.0 collective-permute-done.9
  25.4 0.6 %add.23 = f32[2,16]{1,0:T(2,128)} add(f32[2,16]{1,0:T(2,128)S(1)} %collective-permute-done.8, f32[2,16]{1,0:T(2,128)S(1)} %collective-permute-done.9) | non-fusion elementwise | flops 32 | bytes 384 | tf_op jit(solution)/shard_map/add | solution.py:195
  (4 shorter events, 0.0 us)
Async XLA Ops:
  0.0 16.7 %copy-start.2 = (s32[1,16]{1,0:T(1,128)S(1)}, s32[1,16]{1,0:T(1,128)}, u32[]{:S(2)}) copy-start(s32[1,16]{1,0:T(1,128)} %param.8) | copy-start | bytes 196
  0.0 16.7 %copy-start = (bf16[1,8,2,256,256]{4,3,2,1,0:T(8,128)(2,1)S(1)}, bf16[1,8,2,256,256]{4,3,2,1,0:T(8,128)(2,1)}, u32[]{:S(2)}) copy-start(bf16[1,8,2,256,256]{4,3,2,1,0:T(8,128)(2,1)} %elem_ref.1) | copy-start | bytes 6291460
  2.2 15.8 %copy-start.1 = (s32[1,16]{1,0:T(1,128)S(1)}, s32[1,16]{1,0:T(1,128)}, u32[]{:S(2)}) copy-start(s32[1,16]{1,0:T(1,128)} %mom_ref.1) | copy-start | bytes 196
  2.2 5.3 %collective-permute-start = (bf16[2,64,256]{2,1,0:T(8,128)(2,1)S(1)}, bf16[2,64,256]{2,1,0:T(8,128)(2,1)S(1)}, u32[]{:S(2)}, u32[]{:S(2)}) collective-permute-start(bf16[2,64,256]{2,1,0:T(8,128)(2,1)S(1)} %get-tuple-element.12), channel_id=1, source_target_pairs={{0,1},{1,0},{2,3},{3,2},{4,5},{5,4},{6,7},{7,6},{8,9},{9,8},{10,11... | collective-permute-start | bytes 196616 | tf_op jit(solution)/shard_map/ppermute | solution.py:172
  7.5 4.6 %collective-permute-start.1 = (bf16[1,2,64,256]{3,2,1,0:T(8,128)(2,1)S(1)}, bf16[1,2,64,256]{3,2,1,0:T(8,128)(2,1)S(1)}, u32[]{:S(2)}, u32[]{:S(2)}) collective-permute-start(bf16[1,2,64,256]{3,2,1,0:T(8,128)(2,1)S(1)} %bitcast.4), channel_id=1, source_target_pairs={{0,8},{1,9},{2,10},{3,11},{4,20},{5,21},{6,22},{7,23},{8,0},{9,1},... | collective-permute-start | bytes 196616 | tf_op jit(solution)/shard_map/ppermute | solution.py:172
  9.5 5.2 %collective-permute-start.2 = (bf16[2,64,256]{2,1,0:T(8,128)(2,1)S(1)}, bf16[2,64,256]{2,1,0:T(8,128)(2,1)S(1)}, u32[]{:S(2)}, u32[]{:S(2)}) collective-permute-start(bf16[2,64,256]{2,1,0:T(8,128)(2,1)S(1)} %get-tuple-element.17), channel_id=1, source_target_pairs={{0,2},{1,3},{2,0},{3,1},{4,6},{5,7},{6,4},{7,5},{8,10},{9,11},{10,... | collective-permute-start | bytes 196616 | tf_op jit(solution)/shard_map/ppermute | solution.py:172
  12.2 4.4 %collective-permute-start.3 = (bf16[2,2,64,256]{3,2,1,0:T(8,128)(2,1)S(1)}, bf16[2,2,64,256]{3,2,1,0:T(8,128)(2,1)S(1)}, u32[]{:S(2)}, u32[]{:S(2)}) collective-permute-start(bf16[2,2,64,256]{3,2,1,0:T(8,128)(2,1)S(1)} %pad_maximum_fusion.refs_0_), channel_id=1, source_target_pairs={{0,20},{1,21},{2,22},{3,23},{4,8},{5,9},{6,10},{7,11},{8,28},{9,29... | collective-permute-start | bytes 393224 | tf_op jit(solution)/shard_map/ppermute | solution.py:172
  14.7 1.9 %collective-permute-start.4 = (bf16[2,2,64,256]{3,2,1,0:T(8,128)(2,1)S(1)}, bf16[2,2,64,256]{3,2,1,0:T(8,128)(2,1)S(1)}, u32[]{:S(2)}, u32[]{:S(2)}) collective-permute-start(bf16[2,2,64,256]{3,2,1,0:T(8,128)(2,1)S(1)} %pad_maximum_fusion.refs_0_), channel_id=1, source_target_pairs={{0,4},{1,5},{2,6},{3,7},{4,0},{5,1},{6,2},{7,3},{8,12},{9,13},{10,... | collective-permute-start | bytes 393224 | tf_op jit(solution)/shard_map/ppermute | solution.py:172
  16.6 1.3 %collective-permute-start.5 = (bf16[2,2,64,256]{3,2,1,0:T(8,128)(2,1)S(1)}, bf16[2,2,64,256]{3,2,1,0:T(8,128)(2,1)S(1)}, u32[]{:S(2)}, u32[]{:S(2)}) collective-permute-start(bf16[2,2,64,256]{3,2,1,0:T(8,128)(2,1)S(1)} %collective-permute-done.3.refs_1_), channel_id=1, source_target_pairs={{0,4},{1,5},{2,6},{3,7},{4,0},{5,1},{6,2},{7,3},{8,12},{9,13},{10,... | collective-permute-start | bytes 393224 | tf_op jit(solution)/shard_map/ppermute | solution.py:172
  18.5 3.0 %collective-permute-start.6 = (f32[2,16]{1,0:T(2,128)S(1)}, f32[2,16]{1,0:T(2,128)S(1)}, u32[]{:S(2)}, u32[]{:S(2)}) collective-permute-start(f32[2,16]{1,0:T(2,128)S(1)} %trace.1), channel_id=1, source_target_pairs={{0,5},{1,4},{2,7},{3,6},{4,1},{5,0},{6,3},{7,2},{8,13},{9,12},{10,... | collective-permute-start | bytes 392 | tf_op jit(solution)/shard_map/ppermute | solution.py:172
  20.1 1.5 %collective-permute-start.7 = (f32[2,16]{1,0:T(2,128)S(1)}, f32[2,16]{1,0:T(2,128)S(1)}, u32[]{:S(2)}, u32[]{:S(2)}) collective-permute-start(f32[2,16]{1,0:T(2,128)S(1)} %trace.1), channel_id=1, source_target_pairs={{0,4},{1,5},{2,6},{3,7},{4,0},{5,1},{6,2},{7,3},{8,12},{9,13},{10,... | collective-permute-start | bytes 392 | tf_op jit(solution)/shard_map/ppermute | solution.py:172
  21.5 3.9 %collective-permute-start.8 = (f32[2,16]{1,0:T(2,128)S(1)}, f32[2,16]{1,0:T(2,128)S(1)}, u32[]{:S(2)}, u32[]{:S(2)}) collective-permute-start(f32[2,16]{1,0:T(2,128)S(1)} %add.22), channel_id=1, source_target_pairs={{0,6},{1,7},{2,4},{3,5},{4,2},{5,3},{6,0},{7,1},{8,14},{9,15},{10,... | collective-permute-start | bytes 392 | tf_op jit(solution)/shard_map/ppermute | solution.py:172
  24.1 1.4 %collective-permute-start.9 = (f32[2,16]{1,0:T(2,128)S(1)}, f32[2,16]{1,0:T(2,128)S(1)}, u32[]{:S(2)}, u32[]{:S(2)}) collective-permute-start(f32[2,16]{1,0:T(2,128)S(1)} %add.22), channel_id=1, source_target_pairs={{0,4},{1,5},{2,6},{3,7},{4,0},{5,1},{6,2},{7,3},{8,12},{9,13},{10,... | collective-permute-start | bytes 392 | tf_op jit(solution)/shard_map/ppermute | solution.py:172

commit v8 on v7

--- a/solution.py
+++ b/solution.py
@@ -190,7 +190,7 @@
     groups = [blocks, arrived, swapped, exchange(arrived, cross)]
     mixed = mix(own, other, elementals)
     partial = trace(slots_of(orders, sink_times), momenta, mixed, groups)
-    for bit in range(space_bits):
+    for bit in reversed(range(space_bits)):
         far = exchange(partial, lambda t, s: (t ^ 1, s ^ (1 << bit)))
         partial = far + exchange(partial, cross)
     return partial[:, None, :]

time: 26.2 us -> 26.2 us (level)
  no operation moved by 1% of the time
where the time goes in v8:
time: 26.2 us; the launch traced here: 26 us
  starting transfers between devices  12.6 us (48%)
  waiting for transfers between devices  9.22 us (35%)
  Pallas kernels  3.49 us (13%)
  other arithmetic  0.61 us (2%)
    ppermute x10, starting transfers between devices, exchange(): return lax.ppermute(value, axes, pairs)  12.6 us
    ppermute x10, waiting for transfers between devices, exchange(): return lax.ppermute(value, axes, pairs)  9.22 us
    pallas_call x1, Pallas kernels, project(): pl.pallas_call(project_kernel, out_shape=(jax.ShapeDtypeStruct(shape, jnp...  2.16 us
    pallas_call x1, Pallas kernels, mix(): pl.pallas_call(mix_kernel, out_shape=jax.ShapeDtypeStruct((momenta,) + ow...  0.74 us
    pallas_call x1, Pallas kernels, trace(): pl.pallas_call(trace_kernel, out_shape=jax.ShapeDtypeStruct((2, items), j...  0.59 us
    add x2, other arithmetic, by_exchanges(): partial = far + exchange(partial, cross)  0.57 us
  transfers between devices with their start and end apart: 10, of which 6 were waited for; matrix products, arithmetic and copies ran while one was open for 0% of the time, Pallas kernels for 3%

profile of v8, /device:TPU:0, one launch (start us, length us, event | category | flops | bytes accessed | tf_op | source)
XLA Modules:
  0.0 26.0 jit_solution(5491970754207660462)
XLA Ops:
  0.0 0.0 copy-start.2
  0.0 0.0 copy-start
  0.0 2.2 %project.1 = (f32[2,64,256]{2,1,0:T(8,128)S(1)}, bf16[2,64,256]{2,1,0:T(8,128)(2,1)S(1)}) custom-call(bf16[2,3,1,512,256]{4,3,2,1,0:T(8,128)(2,1)} %vec_hbm.1, bf16[2,3,1,512,128]{4,3,2,1,0:T(8,128)(2,1)} %prop_hbm.1), custom_call_target="tpu_custom_call" | custom-call | tf_op jit(solution)/shard_map/project/pallas_call | solution.py:51
  2.2 0.0 copy-start.1
  2.2 3.1 %collective-permute-start = (bf16[2,64,256]{2,1,0:T(8,128)(2,1)S(1)}, bf16[2,64,256]{2,1,0:T(8,128)(2,1)S(1)}, u32[]{:S(2)}, u32[]{:S(2)}) collective-permute-start(bf16[2,64,256]{2,1,0:T(8,128)(2,1)S(1)} %get-tuple-element.12), channel_id=1, source_target_pairs={{0,1},{1,0},{2,3},{3,2},{4,5},{5,4},{6,7},{7,6},{8,9},{9,8},{10,11... | collective-permute-start | bytes 196616 | tf_op jit(solution)/shard_map/ppermute | solution.py:172
  5.3 2.2 %collective-permute-done = bf16[2,64,256]{2,1,0:T(8,128)(2,1)S(1)} collective-permute-done((bf16[2,64,256]{2,1,0:T(8,128)(2,1)S(1)}, bf16[2,64,256]{2,1,0:T(8,128)(2,1)S(1)}, u32[]{:S(2)}, u32[]{:S(2)}) %collective-permute-start) | collective-permute-done | bytes 65568 | tf_op jit(solution)/shard_map/ppermute | solution.py:172
  7.5 2.0 %collective-permute-start.1 = (bf16[1,2,64,256]{3,2,1,0:T(8,128)(2,1)S(1)}, bf16[1,2,64,256]{3,2,1,0:T(8,128)(2,1)S(1)}, u32[]{:S(2)}, u32[]{:S(2)}) collective-permute-start(bf16[1,2,64,256]{3,2,1,0:T(8,128)(2,1)S(1)} %bitcast.4), channel_id=1, source_target_pairs={{0,8},{1,9},{2,10},{3,11},{4,20},{5,21},{6,22},{7,23},{8,0},{9,1},... | collective-permute-start | bytes 196616 | tf_op jit(solution)/shard_map/ppermute | solution.py:172
  9.5 2.6 %collective-permute-start.2 = (bf16[2,64,256]{2,1,0:T(8,128)(2,1)S(1)}, bf16[2,64,256]{2,1,0:T(8,128)(2,1)S(1)}, u32[]{:S(2)}, u32[]{:S(2)}) collective-permute-start(bf16[2,64,256]{2,1,0:T(8,128)(2,1)S(1)} %get-tuple-element.17), channel_id=1, source_target_pairs={{0,2},{1,3},{2,0},{3,1},{4,6},{5,7},{6,4},{7,5},{8,10},{9,11},{10,... | collective-permute-start | bytes 196616 | tf_op jit(solution)/shard_map/ppermute | solution.py:172
  12.1 0.0 collective-permute-done.1
  12.2 0.1 collective-permute-start.3
  12.2 2.5 %collective-permute-done.2.other_ref = bf16[2,64,256]{2,1,0:T(8,128)(2,1)S(1)} collective-permute-done((bf16[2,64,256]{2,1,0:T(8,128)(2,1)S(1)}, bf16[2,64,256]{2,1,0:T(8,128)(2,1)S(1)}, u32[]{:S(2)}, u32[]{:S(2)}) %collective-permute-start.2) | collective-permute-done | bytes 65568 | tf_op jit(solution)/shard_map/ppermute | solution.py:172
  14.7 0.0 collective-permute-start.4
  14.7 1.9 %collective-permute-done.3.refs_1_ = bf16[2,2,64,256]{3,2,1,0:T(8,128)(2,1)S(1)} collective-permute-done((bf16[2,2,64,256]{3,2,1,0:T(8,128)(2,1)S(1)}, bf16[2,2,64,256]{3,2,1,0:T(8,128)(2,1)S(1)}, u32[]{:S(2)}, u32[]{:S(2)}) %collective-permute-start.3) | collective-permute-done | bytes 131104 | tf_op jit(solution)/shard_map/ppermute | solution.py:172
  16.6 0.0 collective-permute-done.4.refs_2_
  16.6 0.1 collective-permute-start.5
  16.7 0.0 copy-done.2
  16.7 0.0 copy-done
  16.7 0.7 %mix.1.mixed_ref = f32[8,2,64,256]{3,2,1,0:T(8,128)S(1)} custom-call(f32[2,64,256]{2,1,0:T(8,128)S(1)} %get-tuple-element.18.own_ref, bf16[2,64,256]{2,1,0:T(8,128)(2,1)S(1)} %collective-permute-done.2.other_ref, bf16[1,8,2,256,256]{4,3,2,1,0:T(8,128)(2,1)S(1)} %copy-done), custom_call_target="tpu_custom_call" | custom-call | flops 268435456 | bytes 262144 | tf_op jit(solution)/shard_map/mix/pallas_call | solution.py:94
  17.5 0.5 %collective-permute-done.5.refs_3_ = bf16[2,2,64,256]{3,2,1,0:T(8,128)(2,1)S(1)} collective-permute-done((bf16[2,2,64,256]{3,2,1,0:T(8,128)(2,1)S(1)}, bf16[2,2,64,256]{3,2,1,0:T(8,128)(2,1)S(1)}, u32[]{:S(2)}, u32[]{:S(2)}) %collective-permute-start.5) | collective-permute-done | bytes 131104 | tf_op jit(solution)/shard_map/ppermute | solution.py:172
  18.0 0.0 copy-done.1
  18.0 0.6 %trace.1 = f32[2,16]{1,0:T(2,128)S(1)} custom-call(s32[1,16]{1,0:T(1,128)S(1)} %shift-left_add_fusion.slot_ref, s32[1,16]{1,0:T(1,128)S(1)} %copy-done.1, f32[8,2,64,256]{3,2,1,0:T(8,128)S(1)} %mix.1.mixed_ref, bf16[2,2,64,256]{3,2,1,0:T(8,128)(2,1)S(1)} %pad_maximum_fusion.refs_0_, bf16[2,2,64,256]{3,2,1,0:T(8,128)(2,1)S(1)} %collective-permute-done.3.refs_1_, ...), custom_call_target="tpu_custom_call" | custom-call | tf_op jit(solution)/shard_map/trace/pallas_call | solution.py:131
  18.5 2.5 %collective-permute-start.6 = (f32[2,16]{1,0:T(2,128)S(1)}, f32[2,16]{1,0:T(2,128)S(1)}, u32[]{:S(2)}, u32[]{:S(2)}) collective-permute-start(f32[2,16]{1,0:T(2,128)S(1)} %trace.1), channel_id=1, source_target_pairs={{0,6},{1,7},{2,4},{3,5},{4,2},{5,3},{6,0},{7,1},{8,14},{9,15},{10,... | collective-permute-start | bytes 392 | tf_op jit(solution)/shard_map/ppermute | solution.py:172
  21.1 0.4 %collective-permute-start.7 = (f32[2,16]{1,0:T(2,128)S(1)}, f32[2,16]{1,0:T(2,128)S(1)}, u32[]{:S(2)}, u32[]{:S(2)}) collective-permute-start(f32[2,16]{1,0:T(2,128)S(1)} %trace.1), channel_id=1, source_target_pairs={{0,4},{1,5},{2,6},{3,7},{4,0},{5,1},{6,2},{7,3},{8,12},{9,13},{10,... | collective-permute-start | bytes 392 | tf_op jit(solution)/shard_map/ppermute | solution.py:172
  21.4 1.0 %collective-permute-done.6 = f32[2,16]{1,0:T(2,128)S(1)} collective-permute-done((f32[2,16]{1,0:T(2,128)S(1)}, f32[2,16]{1,0:T(2,128)S(1)}, u32[]{:S(2)}, u32[]{:S(2)}) %collective-permute-start.6) | collective-permute-done | bytes 160 | tf_op jit(solution)/shard_map/ppermute | solution.py:172
  22.4 0.0 collective-permute-done.7
  22.4 1.5 %collective-permute-start.8 = (f32[2,16]{1,0:T(2,128)S(1)}, f32[2,16]{1,0:T(2,128)S(1)}, u32[]{:S(2)}, u32[]{:S(2)}) collective-permute-start(f32[2,16]{1,0:T(2,128)S(1)} %add.22), channel_id=1, source_target_pairs={{0,5},{1,4},{2,7},{3,6},{4,1},{5,0},{6,3},{7,2},{8,13},{9,12},{10,... | collective-permute-start | bytes 392 | tf_op jit(solution)/shard_map/ppermute | solution.py:172
  24.0 0.4 %collective-permute-start.9 = (f32[2,16]{1,0:T(2,128)S(1)}, f32[2,16]{1,0:T(2,128)S(1)}, u32[]{:S(2)}, u32[]{:S(2)}) collective-permute-start(f32[2,16]{1,0:T(2,128)S(1)} %add.22), channel_id=1, source_target_pairs={{0,4},{1,5},{2,6},{3,7},{4,0},{5,1},{6,2},{7,3},{8,12},{9,13},{10,... | collective-permute-start | bytes 392 | tf_op jit(solution)/shard_map/ppermute | solution.py:172
  24.3 1.1 %collective-permute-done.8 = f32[2,16]{1,0:T(2,128)S(1)} collective-permute-done((f32[2,16]{1,0:T(2,128)S(1)}, f32[2,16]{1,0:T(2,128)S(1)}, u32[]{:S(2)}, u32[]{:S(2)}) %collective-permute-start.8) | collective-permute-done | bytes 160 | tf_op jit(solution)/shard_map/ppermute | solution.py:172
  25.4 0.0 collective-permute-done.9
  25.4 0.6 %add.23 = f32[2,16]{1,0:T(2,128)} add(f32[2,16]{1,0:T(2,128)S(1)} %collective-permute-done.8, f32[2,16]{1,0:T(2,128)S(1)} %collective-permute-done.9) | non-fusion elementwise | flops 32 | bytes 384 | tf_op jit(solution)/shard_map/add | solution.py:195
  (4 shorter events, 0.0 us)
Async XLA Ops:
  0.0 16.7 %copy-start.2 = (s32[1,16]{1,0:T(1,128)S(1)}, s32[1,16]{1,0:T(1,128)}, u32[]{:S(2)}) copy-start(s32[1,16]{1,0:T(1,128)} %param.8) | copy-start | bytes 196
  0.0 16.7 %copy-start = (bf16[1,8,2,256,256]{4,3,2,1,0:T(8,128)(2,1)S(1)}, bf16[1,8,2,256,256]{4,3,2,1,0:T(8,128)(2,1)}, u32[]{:S(2)}) copy-start(bf16[1,8,2,256,256]{4,3,2,1,0:T(8,128)(2,1)} %elem_ref.1) | copy-start | bytes 6291460
  2.2 15.8 %copy-start.1 = (s32[1,16]{1,0:T(1,128)S(1)}, s32[1,16]{1,0:T(1,128)}, u32[]{:S(2)}) copy-start(s32[1,16]{1,0:T(1,128)} %mom_ref.1) | copy-start | bytes 196
  2.2 5.3 %collective-permute-start = (bf16[2,64,256]{2,1,0:T(8,128)(2,1)S(1)}, bf16[2,64,256]{2,1,0:T(8,128)(2,1)S(1)}, u32[]{:S(2)}, u32[]{:S(2)}) collective-permute-start(bf16[2,64,256]{2,1,0:T(8,128)(2,1)S(1)} %get-tuple-element.12), channel_id=1, source_target_pairs={{0,1},{1,0},{2,3},{3,2},{4,5},{5,4},{6,7},{7,6},{8,9},{9,8},{10,11... | collective-permute-start | bytes 196616 | tf_op jit(solution)/shard_map/ppermute | solution.py:172
  7.5 4.6 %collective-permute-start.1 = (bf16[1,2,64,256]{3,2,1,0:T(8,128)(2,1)S(1)}, bf16[1,2,64,256]{3,2,1,0:T(8,128)(2,1)S(1)}, u32[]{:S(2)}, u32[]{:S(2)}) collective-permute-start(bf16[1,2,64,256]{3,2,1,0:T(8,128)(2,1)S(1)} %bitcast.4), channel_id=1, source_target_pairs={{0,8},{1,9},{2,10},{3,11},{4,20},{5,21},{6,22},{7,23},{8,0},{9,1},... | collective-permute-start | bytes 196616 | tf_op jit(solution)/shard_map/ppermute | solution.py:172
  9.5 5.2 %collective-permute-start.2 = (bf16[2,64,256]{2,1,0:T(8,128)(2,1)S(1)}, bf16[2,64,256]{2,1,0:T(8,128)(2,1)S(1)}, u32[]{:S(2)}, u32[]{:S(2)}) collective-permute-start(bf16[2,64,256]{2,1,0:T(8,128)(2,1)S(1)} %get-tuple-element.17), channel_id=1, source_target_pairs={{0,2},{1,3},{2,0},{3,1},{4,6},{5,7},{6,4},{7,5},{8,10},{9,11},{10,... | collective-permute-start | bytes 196616 | tf_op jit(solution)/shard_map/ppermute | solution.py:172
  12.2 4.4 %collective-permute-start.3 = (bf16[2,2,64,256]{3,2,1,0:T(8,128)(2,1)S(1)}, bf16[2,2,64,256]{3,2,1,0:T(8,128)(2,1)S(1)}, u32[]{:S(2)}, u32[]{:S(2)}) collective-permute-start(bf16[2,2,64,256]{3,2,1,0:T(8,128)(2,1)S(1)} %pad_maximum_fusion.refs_0_), channel_id=1, source_target_pairs={{0,20},{1,21},{2,22},{3,23},{4,8},{5,9},{6,10},{7,11},{8,28},{9,29... | collective-permute-start | bytes 393224 | tf_op jit(solution)/shard_map/ppermute | solution.py:172
  14.7 1.9 %collective-permute-start.4 = (bf16[2,2,64,256]{3,2,1,0:T(8,128)(2,1)S(1)}, bf16[2,2,64,256]{3,2,1,0:T(8,128)(2,1)S(1)}, u32[]{:S(2)}, u32[]{:S(2)}) collective-permute-start(bf16[2,2,64,256]{3,2,1,0:T(8,128)(2,1)S(1)} %pad_maximum_fusion.refs_0_), channel_id=1, source_target_pairs={{0,4},{1,5},{2,6},{3,7},{4,0},{5,1},{6,2},{7,3},{8,12},{9,13},{10,... | collective-permute-start | bytes 393224 | tf_op jit(solution)/shard_map/ppermute | solution.py:172
  16.6 1.3 %collective-permute-start.5 = (bf16[2,2,64,256]{3,2,1,0:T(8,128)(2,1)S(1)}, bf16[2,2,64,256]{3,2,1,0:T(8,128)(2,1)S(1)}, u32[]{:S(2)}, u32[]{:S(2)}) collective-permute-start(bf16[2,2,64,256]{3,2,1,0:T(8,128)(2,1)S(1)} %collective-permute-done.3.refs_1_), channel_id=1, source_target_pairs={{0,4},{1,5},{2,6},{3,7},{4,0},{5,1},{6,2},{7,3},{8,12},{9,13},{10,... | collective-permute-start | bytes 393224 | tf_op jit(solution)/shard_map/ppermute | solution.py:172
  18.5 3.9 %collective-permute-start.6 = (f32[2,16]{1,0:T(2,128)S(1)}, f32[2,16]{1,0:T(2,128)S(1)}, u32[]{:S(2)}, u32[]{:S(2)}) collective-permute-start(f32[2,16]{1,0:T(2,128)S(1)} %trace.1), channel_id=1, source_target_pairs={{0,6},{1,7},{2,4},{3,5},{4,2},{5,3},{6,0},{7,1},{8,14},{9,15},{10,... | collective-permute-start | bytes 392 | tf_op jit(solution)/shard_map/ppermute | solution.py:172
  21.1 1.4 %collective-permute-start.7 = (f32[2,16]{1,0:T(2,128)S(1)}, f32[2,16]{1,0:T(2,128)S(1)}, u32[]{:S(2)}, u32[]{:S(2)}) collective-permute-start(f32[2,16]{1,0:T(2,128)S(1)} %trace.1), channel_id=1, source_target_pairs={{0,4},{1,5},{2,6},{3,7},{4,0},{5,1},{6,2},{7,3},{8,12},{9,13},{10,... | collective-permute-start | bytes 392 | tf_op jit(solution)/shard_map/ppermute | solution.py:172
  22.4 3.0 %collective-permute-start.8 = (f32[2,16]{1,0:T(2,128)S(1)}, f32[2,16]{1,0:T(2,128)S(1)}, u32[]{:S(2)}, u32[]{:S(2)}) collective-permute-start(f32[2,16]{1,0:T(2,128)S(1)} %add.22), channel_id=1, source_target_pairs={{0,5},{1,4},{2,7},{3,6},{4,1},{5,0},{6,3},{7,2},{8,13},{9,12},{10,... | collective-permute-start | bytes 392 | tf_op jit(solution)/shard_map/ppermute | solution.py:172
  24.0 1.5 %collective-permute-start.9 = (f32[2,16]{1,0:T(2,128)S(1)}, f32[2,16]{1,0:T(2,128)S(1)}, u32[]{:S(2)}, u32[]{:S(2)}) collective-permute-start(f32[2,16]{1,0:T(2,128)S(1)} %add.22), channel_id=1, source_target_pairs={{0,4},{1,5},{2,6},{3,7},{4,0},{5,1},{6,2},{7,3},{8,12},{9,13},{10,... | collective-permute-start | bytes 392 | tf_op jit(solution)/shard_map/ppermute | solution.py:172
